TPU v7x, 128 devices: a whole 4x4x4 slice. The times are simulated.
128 devices in a mesh: lat: 4 (over z_hi, core), lon: 32 (over x, y, z_lo).
Axes of the slice: x: 4, y: 4, z: 4 (z_hi: 2, z_lo: 2; z = z_hi * 2 + z_lo), core: 2. Of those that a mesh axis runs over, the one named last changes fastest.
Arguments:
- terrain_surface: float32 [1024, 32768], P('lat', 'lon')
- azimuth_lag_tallies: int32 [8, 8], replicated, may hold values from 1 to 128, as said below
- holder_devices: int32 [524288, 1], P(('lat', 'lon')), may hold values from 0 to 127; in each aligned block of 4096 rows (0 to 4095, 4096 to 8191, ...) at most 128 rows name the same one
- holder_region_slot: int32 [524288], P(('lat', 'lon')), may hold values from 0 to 511
- footprint_weight: int32 [524288], P(('lat', 'lon')), may hold values from 1 to 64
Outputs:
- fine_svf: float32 [1024, 32768], P('lat', 'lon')
- cell_horizon: float32 [8, 65536], P(None, ('lat', 'lon'))
- cell_svf: float32 [65536], P(('lat', 'lon'))
Inputs may be any that keep to these rules, and one draw needn't show every extreme that they name: `holder_devices`: in the blocks of one device no owner is named by more than 128 blocks, a bound that some block reaches. `azimuth_lag_tallies`: every azimuth has a distance of 128.
All inputs are finite; a program needn't handle non-finite values.
Results may differ from a plain program's by a relative error of at most 0.0003.
Values sent between devices are 32-bit elements; how exact they have to be, the bound alone decides.
No kernel may reach another device: no remote copies, remote signals or barrier semaphores. Data moves between devices by JAX's collectives and lax.ppermute only.
A program may use at most 192 MiB of HBM per device.

v0:
```python
import jax
import jax.numpy as jnp
from jax import lax
from jax.experimental import pallas as pl
from jax.experimental.pallas import tpu as pltpu

FARTHEST_LAG = 128
AZ = 8
KS = 8
pixel_size = 92.6
ATAN = (0.9999999, -0.33331991, 0.19969724, -0.14019481, 0.09914293, -0.05948639, 0.0242524, -0.00469327)
HALF_PI = 1.5707963267948966


def recip(v):
    g = pl.reciprocal(v, approx=True)
    return g * (2.0 - v * g)


def angle(x, y):
    ax, ay = jnp.abs(x), jnp.abs(y)
    z = jnp.minimum(ax, ay) * recip(jnp.maximum(ax, ay))
    u = z * z
    p = ATAN[7]
    for c in ATAN[6::-1]:
        p = p * u + c
    p = p * z
    p = jnp.where(ay > ax, HALF_PI - p, p)
    p = jnp.where(x < 0.0, 2.0 * HALF_PI - p, p)
    return jnp.where(y < 0.0, 4.0 * HALF_PI - p, p)


N_DEV = 128
NBR = 32
CELLS_DEV = 512
F32 = jnp.float32
BF16 = jnp.bfloat16
VMEM = pl.BlockSpec(memory_space=pltpu.VMEM)
SMEM = pl.BlockSpec(memory_space=pltpu.SMEM)
ANY = pl.BlockSpec(memory_space=pl.ANY)
NT = (((1,), (1,)), ((), ()))


def split2(v):
    hi = v.astype(BF16)
    return hi, (v - hi.astype(F32)).astype(BF16)


def iota(shape, dim):
    return lax.broadcasted_iota(jnp.int32, shape, dim)


def route_kernel(owner_ref, slot_ref, weight_ref, start_ref, index_ref, meta_ref, rank_ref):
    sub = iota((N_DEV, 128), 0)
    upper = (iota((128, 128), 0) < iota((128, 128), 1)).astype(BF16)
    right = jnp.concatenate([upper, jnp.ones((128, 128), BF16)], axis=1)
    count = jnp.zeros((N_DEV, 128), F32)
    for i in range(NBR):
        mine = sub == owner_ref[i : i + 1, :]
        both = jnp.dot(mine.astype(BF16), right, preferred_element_type=F32)
        rank = jnp.sum(jnp.where(mine, both[:, :128] + count, 0.0), axis=0, keepdims=True)
        rank_ref[i : i + 1, :] = rank
        count = count + both[:, 128:]
    lower = (iota((128, 128), 0) > iota((128, 128), 1)).astype(BF16)
    start = jnp.dot(lower, count.astype(BF16), preferred_element_type=F32)
    start_row = lax.dot_general(count[:, :8].T.astype(BF16), upper, (((1,), (0,)), ((), ())), preferred_element_type=F32)
    start_ref[...] = start_row[:1].astype(jnp.int32)
    meta = jnp.zeros((3 * N_DEV, 128), F32)
    for i in range(NBR):
        mine = sub == owner_ref[i : i + 1, :]
        rank = rank_ref[i : i + 1, :]
        place = (rank + jnp.sum(jnp.where(mine, start, 0.0), axis=0, keepdims=True)).astype(jnp.int32)
        rank = rank.astype(jnp.int32)
        index_ref[i : i + 1, :] = lax.shift_right_logical(place, 7)
        index_ref[NBR + i : NBR + i + 1, :] = lax.bitwise_and(place, 127)
        index_ref[2 * NBR + i : 2 * NBR + i + 1, :] = rank
        rank_hot = (sub == rank).astype(BF16)
        slot = slot_ref[i : i + 1, :] + 1
        parts = (lax.shift_right_logical(slot, 4), lax.bitwise_and(slot, 15), weight_ref[i : i + 1, :])
        left = jnp.concatenate([jnp.where(mine, v.astype(F32), 0.0) for v in parts], axis=0).astype(BF16)
        meta = meta + lax.dot_general(left, rank_hot, NT, preferred_element_type=F32)
    meta_ref[0] = meta[:N_DEV] * 16.0 + meta[N_DEV : 2 * N_DEV]
    meta_ref[1] = meta[2 * N_DEV :]


def route(owner, slot, weight):
    return pl.pallas_call(
        route_kernel,
        name="route",
        out_shape=(
            jax.ShapeDtypeStruct((1, N_DEV), jnp.int32),
            jax.ShapeDtypeStruct((96, 128), jnp.int32),
            jax.ShapeDtypeStruct((2, N_DEV, 128), F32),
        ),
        in_specs=[VMEM] * 3,
        out_specs=[VMEM] * 3,
        scratch_shapes=[pltpu.VMEM((NBR, 128), F32)],
        cost_estimate=pl.CostEstimate(flops=int(4e8), bytes_accessed=200000, transcendentals=0),
    )(owner, slot, weight)


def turned(z, r):
    if z is None:
        return (None, r)
    x, y = z
    if x is None:
        return (1.0 - y * r, y + r)
    return (x - y * r, y + x * r)


def sample(lags, inv_lags, invb, H, h0, it, rays, S_ref, svf_in, svf_out):
    lane = iota((8, 128), 1)
    rc = lax.shift_right_logical(it, 1)
    r0 = rc * 64 + lax.bitwise_and(it, 1) * 4
    for f, (a, sy, sx) in enumerate(rays):
        flat = isinstance(sy, int) and sy == 0
        z = [None] * 8
        off = 1 if sx >= 0 else 0
        count = 8 if sx == 0 else 9
        for p in range(4):
            here = r0 + p
            t = [H[1 + j, pl.ds(h0 + here, 8, stride=8), :] for j in range(8)]
            best = [None] * 8
            if flat:
                far = [H[off + j, pl.ds(h0 + here, 8, stride=8), :] for j in range(count)]
            for k in range(KS):
                s = lags[a, k]
                il = inv_lags[a, k]
                if not flat:
                    row = h0 + here + sy * s
                    far = [H[off + j, pl.ds(row, 8, stride=8), :] for j in range(count)]
                if sx == 0:
                    got = far
                else:
                    amount = 128 - s if sx == 1 else lax.bitwise_and(s, 127)
                    keep = lane < (amount if sx == 1 else s)
                    rolled = [pltpu.roll(v, amount, 1) for v in far]
                    got = [jnp.where(keep, rolled[j], rolled[j + 1]) for j in range(8)]
                for j in range(8):
                    v = (got[j] - t[j]) * il
                    best[j] = v if k == 0 else jnp.maximum(best[j], v)
            ib = 1.0 / pixel_size if sx == 0 else invb[1 if flat else 0, pl.ds(here, 8, stride=8), :]
            for j in range(8):
                rise = jnp.minimum(jnp.maximum(best[j] * ib, 0.0), 1e8)
                z[j] = turned(z[j], rise)
                opening = recip(1.0 + rise * rise)
                if f == 0 and svf_in is not None:
                    opening = opening + svf_in[j, pl.ds(here, 8, stride=8), :]
                if f > 0:
                    opening = opening + svf_out[j, pl.ds(here, 8, stride=8), :]
                svf_out[j, pl.ds(here, 8, stride=8), :] = opening
        for j in range(8):
            S_ref[rc, f, j] += angle(*z[j])
    for j in range(8):
        v = [svf_out[j, pl.ds(r0 + p, 8, stride=8), :] for p in range(4)]
        S_ref[rc, len(rays), j] += (v[0] + v[1]) + (v[2] + v[3])


def slanted(southward):
    sy = jnp.where(southward, 1, -1)
    return [(jnp.where(southward, 3, 5), sy, -1), (jnp.where(southward, 2, 6), sy, 0), (jnp.where(southward, 1, 7), sy, 1)]


def copies(pairs, sems):
    made = [pltpu.make_async_copy(a, b, sems.at[i]) for i, (a, b) in enumerate(pairs)]
    for c in made:
        c.start()
    for c in made:
        c.wait()


def cols(j):
    return pl.ds(j * 128, 128)


def inner_kernel(lags, inv_lags, own, west, east, invb, V_ref, S_ref, H, sems):
    copies(
        [(own.at[:, cols(j)], H.at[1 + j]) for j in range(8)] + [(west, H.at[0]), (east, H.at[9])], sems
    )

    S_ref[...] = jnp.zeros(S_ref.shape, F32)

    def step(it, carry):
        rays = [(0, 0, 1), (4, 0, -1)] + slanted(it < 4)
        sample(lags, inv_lags, invb, H, 0, it, rays, S_ref, None, V_ref)
        return carry

    lax.fori_loop(0, 8, step, 0)


def inner(*args):
    return pl.pallas_call(
        inner_kernel,
        name="inner",
        out_shape=(jax.ShapeDtypeStruct((8, 256, 128), F32), jax.ShapeDtypeStruct((4, 6, 8, 8, 128), F32)),
        in_specs=[SMEM] * 2 + [ANY] * 3 + [VMEM],
        out_specs=[VMEM] * 2,
        scratch_shapes=[pltpu.VMEM((10, 256, 128), F32), pltpu.SemaphoreType.DMA((10,))],
        compiler_params=pltpu.CompilerParams(vmem_limit_bytes=24 * 1024 * 1024),
        cost_estimate=pl.CostEstimate(flops=int(4e8), bytes_accessed=30000000, transcendentals=0),
    )(*args)


def outer_kernel(
    lags, inv_lags, starts, lat, own, north, south, west, east, invb, V_in, S_in, weight, owner, index, meta,
    svf_ref, out_ref, H, S, V, R, Z, Y, O, F, acc, sems,
):
    pairs = [(own.at[:, cols(j)], H.at[1 + j, pl.ds(128, 256)]) for j in range(8)]
    pairs += [(west, H.at[0, pl.ds(128, 256)]), (east, H.at[9, pl.ds(128, 256)])]
    pairs += [(north.at[:, cols(j)], H.at[j, pl.ds(0, 128)]) for j in range(10)]
    pairs += [(south.at[:, cols(j)], H.at[j, pl.ds(384, 128)]) for j in range(10)]
    copies(pairs, sems)

    @pl.when(lat[0] == 0)
    def _():
        for c in range(10):
            H[c, 0:128, :] = jnp.broadcast_to(H[c, 128:129, :], (128, 128))

    @pl.when(lat[0] == lat[1] - 1)
    def _():
        for c in range(10):
            H[c, 384:512, :] = jnp.broadcast_to(H[c, 383:384, :], (128, 128))

    S[...] = jnp.zeros(S.shape, F32)

    def step(it, carry):
        sample(lags, inv_lags, invb, H, 128, it, slanted(it >= 4), S, V_in, V)
        return carry

    lax.fori_loop(0, 8, step, 0)
    for j in range(8):
        svf_ref[:, j * 128 : (j + 1) * 128] = V[j] * (1.0 / AZ)

    total = jnp.zeros((288, 128), F32)
    for j in range(8):
        pool = (iota((128, 128), 1) == j * 16 + lax.shift_right_logical(iota((128, 128), 0), 3)).astype(BF16)
        field = []
        for rc in range(4):
            here, there = ((S_in, 2), (S, 0)) if rc < 2 else ((S, 0), (S_in, 2))
            where = [(S_in, 0), (here[0], here[1] + 2), (here[0], here[1] + 1), (here[0], here[1])]
            where += [(S_in, 1), (there[0], there[1]), (there[0], there[1] + 1), (there[0], there[1] + 2), (S, 3)]
            field += [ref[rc, f, j] for ref, f in where]
        hi, lo = split2(jnp.concatenate(field, axis=0))
        total = total + jnp.dot(hi, pool, preferred_element_type=F32) + jnp.dot(lo, pool, preferred_element_type=F32)
    R[...] = total
    lane = iota((8, 128), 1)
    scale = 1.0 / 4096.0
    for rc in range(4):
        for i in range(8):
            b = rc * 8 + i
            Y[b] = R[pl.ds(rc * 72 + i, 8, stride=8), :] * (weight[b : b + 1, :].astype(F32) * scale)
        O[rc * 8 : rc * 8 + 8, :] = R[rc * 72 + 64 : rc * 72 + 72, :] * (weight[rc * 8 : rc * 8 + 8, :].astype(F32) * (scale / AZ))

    acc[...] = jnp.zeros(acc.shape, F32)
    low = iota((128, 512), 0).astype(F32).astype(BF16)
    zero = jnp.zeros((16, 512), BF16)

    def wide(ref, row):
        return jnp.concatenate([ref[pl.ds(row + i, 1), :] for i in range(4)], axis=1)

    def sort(g, carry):
        b = g * 4
        v = jnp.concatenate([Y[b + i] for i in range(4)], axis=1)
        v = jnp.concatenate(split2(v), axis=0)
        o_hi, o_lo = split2(jnp.broadcast_to(wide(O, b), (128, 512)))
        tile = jnp.broadcast_to(wide(index, b).astype(F32), (16, 512)).astype(BF16)
        left = [jnp.where(tile == BF16(t), v, zero) for t in range(NBR)]
        hot = (low == jnp.broadcast_to(wide(index, 32 + b).astype(F32), (128, 512)).astype(BF16)).astype(BF16)
        acc[0:512, :] += lax.dot_general(jnp.concatenate(left, axis=0), hot, NT, preferred_element_type=F32)
        mine = low == jnp.broadcast_to(wide(owner, b).astype(F32), (128, 512)).astype(BF16)
        hot = (low == jnp.broadcast_to(wide(index, 64 + b).astype(F32), (128, 512)).astype(BF16)).astype(BF16)
        left = [jnp.where(mine, o_hi, jnp.zeros_like(o_hi)), jnp.where(mine, o_lo, jnp.zeros_like(o_lo))]
        acc[512:768, :] += lax.dot_general(jnp.concatenate(left, axis=0), hot, NT, preferred_element_type=F32)
        return carry

    lax.fori_loop(0, NBR // 4, sort, 0, unroll=2)
    for t in range(NBR):
        Z[t] = acc[t * 16 : t * 16 + 8, :] + acc[t * 16 + 8 : t * 16 + 16, :]
    Z[32] = jnp.zeros((8, 128), F32)
    out_ref[:, 8 * 128 : 9 * 128] = acc[512:640, :] + acc[640:768, :]

    def expand(o, carry):
        st = starts[0, o]
        tile = lax.shift_right_logical(st, 7)
        q = 128 - lax.bitwise_and(st, 127)
        amount = lax.bitwise_and(q, 127)
        after = jnp.minimum(tile + 1, 32)
        tile = jnp.minimum(tile, 32)
        keep = lane < q
        a = pltpu.roll(Z[tile], amount, 1)
        b = pltpu.roll(Z[after], amount, 1)
        F[pl.ds(o, 8, stride=N_DEV), :] = jnp.where(keep, a, b)
        return carry

    lax.fori_loop(0, N_DEV, expand, 0, unroll=8)
    for f in range(8):
        out_ref[:, f * 128 : (f + 1) * 128] = F[f * N_DEV : (f + 1) * N_DEV, :]
    out_ref[:, 9 * 128 : 10 * 128] = meta[0]
    out_ref[:, 10 * 128 : 11 * 128] = meta[1]


def outer(*args):
    return pl.pallas_call(
        outer_kernel,
        name="outer",
        out_shape=(jax.ShapeDtypeStruct((256, 1024), F32), jax.ShapeDtypeStruct((N_DEV, 11 * 128), F32)),
        in_specs=[SMEM] * 4 + [ANY] * 5 + [VMEM] * 7,
        out_specs=[VMEM] * 2,
        scratch_shapes=[
            pltpu.VMEM((10, 512, 128), F32),
            pltpu.VMEM((4, 4, 8, 8, 128), F32),
            pltpu.VMEM((8, 256, 128), F32),
            pltpu.VMEM((288, 128), F32),
            pltpu.VMEM((33, 8, 128), F32),
            pltpu.VMEM((32, 8, 128), F32),
            pltpu.VMEM((32, 128), F32),
            pltpu.VMEM((8 * N_DEV, 128), F32),
            pltpu.VMEM((768, 128), F32),
            pltpu.SemaphoreType.DMA((30,)),
        ],
        compiler_params=pltpu.CompilerParams(vmem_limit_bytes=32 * 1024 * 1024),
        cost_estimate=pl.CostEstimate(flops=int(4e8), bytes_accessed=20000000, transcendentals=0),
    )(*args)


def cells_kernel(got_ref, horizon_ref, svf_ref, G):
    for f in range(9):
        G[pl.ds(f, N_DEV, stride=16), :] = got_ref[:, f * 128 : (f + 1) * 128]
    cell = got_ref[:, 9 * 128 : 10 * 128].astype(jnp.int32) - 1
    G[pl.ds(9, N_DEV, stride=16), :] = lax.shift_right_arithmetic(cell, 7).astype(F32)
    G[pl.ds(10, N_DEV, stride=16), :] = got_ref[:, 10 * 128 : 11 * 128]
    G[pl.ds(11, N_DEV, stride=16), :] = lax.bitwise_and(cell, 127).astype(F32)
    for f in range(12, 16):
        G[pl.ds(f, N_DEV, stride=16), :] = jnp.zeros((N_DEV, 128), F32)
    low = iota((128, 512), 0).astype(F32).astype(BF16)

    def accumulate(t, acc):
        base = pl.multiple_of(t * 64, 64)
        v = jnp.concatenate([G[pl.ds(base + 16 * i, 16), :] for i in range(4)], axis=1)
        hi, lo = split2(v)
        high = jnp.broadcast_to(v[9:10, :], (16, 512)).astype(BF16)
        zero = jnp.zeros((16, 512), BF16)
        left = []
        for h in range(4):
            mine = high == BF16(h)
            left += [jnp.where(mine, hi, zero), jnp.where(mine, lo, zero)]
        hot = (low == jnp.broadcast_to(v[11:12, :], (128, 512)).astype(BF16)).astype(BF16)
        return acc + lax.dot_general(jnp.concatenate(left, axis=0), hot, NT, preferred_element_type=F32)

    acc = lax.fori_loop(0, N_DEV // 4, accumulate, jnp.zeros((128, 128), F32), unroll=8)
    sums = jnp.concatenate([acc[h * 32 : h * 32 + 16] + acc[h * 32 + 16 : h * 32 + 32] for h in range(4)], axis=1)
    area = jnp.maximum(sums[10:11, :] * (1.0 / 64.0), 1.0)
    horizon_ref[...] = sums[0:8] / area
    svf_ref[...] = sums[8:9] / area


def cells(got):
    return pl.pallas_call(
        cells_kernel,
        name="cells",
        out_shape=(jax.ShapeDtypeStruct((AZ, CELLS_DEV), F32), jax.ShapeDtypeStruct((1, CELLS_DEV), F32)),
        in_specs=[VMEM],
        out_specs=[VMEM] * 2,
        scratch_shapes=[pltpu.VMEM((16 * N_DEV, 128), F32)],
        compiler_params=pltpu.CompilerParams(vmem_limit_bytes=24 * 1024 * 1024),
    )(got)


def shards(terrain_surface, azimuth_lag_tallies, holder_devices, holder_region_slot, footprint_weight):
    rows, width = terrain_surface.shape
    n_lat = lax.axis_size("lat")
    n_lon = lax.axis_size("lon")
    W = FARTHEST_LAG
    own = terrain_surface
    east_pairs = [((i + 1) % n_lon, i) for i in range(n_lon)]
    west = lax.ppermute(own[:, width - W :], "lon", [(j, i) for i, j in east_pairs])
    east = lax.ppermute(own[:, :W], "lon", east_pairs)
    weight = footprint_weight.reshape(NBR, 128)
    owner = holder_devices.reshape(NBR, 128)
    start, index, meta = route(owner, holder_region_slot.reshape(NBR, 128), weight)
    west, east, start, index, meta = lax.optimization_barrier((west, east, start, index, meta))
    wide = jnp.concatenate([west, own, east], axis=1)
    down = [(i, i + 1) for i in range(n_lat - 1)]
    north = lax.ppermute(wide[rows - W :], "lat", down)
    south = lax.ppermute(wide[:W], "lat", [(j, i) for i, j in down])

    rows_global = (lax.axis_index("lat") * rows + jnp.arange(rows, dtype=jnp.int32)).astype(F32)
    latitude = 47.0 - (rows_global + 0.5) / 1200.0
    coslat = jnp.cos(latitude * jnp.pi / 180.0)
    across = (pixel_size * coslat) ** 2
    inv_base = 1.0 / jnp.sqrt(jnp.stack([pixel_size**2 + across, across]))
    inv_base = jnp.broadcast_to(inv_base[:, :, None], (2, rows, 128))
    lat = jnp.stack([lax.axis_index("lat").astype(jnp.int32), jnp.int32(n_lat)])
    inv_lags = 1.0 / azimuth_lag_tallies.astype(F32)
    part, sums = inner(azimuth_lag_tallies, inv_lags, own, west, east, inv_base)
    fine_svf, packed = outer(
        azimuth_lag_tallies, inv_lags, start, lat, own, north, south, west, east, inv_base, part, sums, weight, owner, index, meta
    )
    got = lax.all_to_all(packed, ("lat", "lon"), split_axis=0, concat_axis=0, tiled=True)
    cell_horizon, cell_svf = cells(got)
    return fine_svf, cell_horizon, cell_svf.reshape(CELLS_DEV)


def solution(mesh):
    P = jax.sharding.PartitionSpec
    in_specs = (P("lat", "lon"), P(), P(("lat", "lon"), None), P(("lat", "lon")), P(("lat", "lon")))
    out_specs = (P("lat", "lon"), P(None, ("lat", "lon")), P(("lat", "lon")))
    return jax.shard_map(shards, mesh=mesh, in_specs=in_specs, out_specs=out_specs, check_vma=False)
```

profile of v0, /device:TPU:1, one launch (start us, length us, event | category | flops | bytes accessed | tf_op | source)
XLA Modules:
  0.0 84.7 jit_solution(17747594022884096014)
XLA Ops:
  0.6 0.0 copy-start
  0.6 1.1 %fusion.1 = (f32[256,128]{1,0:T(8,128)S(1)}, f32[256,128]{1,0:T(8,128)S(1)}) fusion(f32[256,1024]{1,0:T(8,128)} %own.3), kind=kLoop, calls=%fused_computation.10 | loop fusion | bytes 524288 | tf_op jit(solution)/shard_map/slice | solution.py:377
  1.7 7.2 %collective-permute-start.1 = (f32[256,128]{1,0:T(8,128)S(1)}, f32[256,128]{1,0:T(8,128)S(1)}, u32[]{:S(2)}, u32[]{:S(2)}) collective-permute-start(f32[256,128]{1,0:T(8,128)S(1)} %get-tuple-element.33), channel_id=1, source_target_pairs={{1,0},{2,1},{3,2},{4,3},{5,4},{6,5},{7,6},{8,7},{9,8},{10,9},{11,1... | collective-permute-start | bytes 393224 | tf_op jit(solution)/shard_map/ppermute | solution.py:377
  8.9 0.0 collective-permute-start
  8.9 3.5 %route.1 = (s32[1,128]{1,0:T(1,128)}, s32[96,128]{1,0:T(8,128)}, f32[2,128,128]{2,1,0:T(8,128)}) custom-call(s32[32,128]{1,0:T(8,128)} %bitcast.11, s32[32,128]{1,0:T(8,128)} %bitcast.15, s32[32,128]{1,0:T(8,128)} %bitcast.13), custom_call_target="tpu_custom_call" | custom-call | flops 400000000 | bytes 200000 | tf_op jit(solution)/shard_map/route/pallas_call | solution.py:87
  12.4 0.0 collective-permute-done.1.east
  12.4 4.5 %collective-permute-done.west = f32[256,128]{1,0:T(8,128)S(1)} collective-permute-done((f32[256,128]{1,0:T(8,128)S(1)}, f32[256,128]{1,0:T(8,128)S(1)}, u32[]{:S(2)}, u32[]{:S(2)}) %collective-permute-start) | collective-permute-done | bytes 131104 | tf_op jit(solution)/shard_map/ppermute | solution.py:376
  17.0 0.0 copy-done
  17.0 0.1 constant_dynamic-update-slice_fusion.1
  17.1 0.0 copy-start.3
  17.1 0.9 %fusion = (f32[128,1280]{1,0:T(8,128)}, f32[128,1280]{1,0:T(8,128)S(1)}) fusion(f32[256,1280]{1,0:T(8,128)S(1)} %constant_dynamic-update-slice_fusion), kind=kLoop, calls=%fused_computation.9 | loop fusion | bytes 2621440 | tf_op jit(solution)/shard_map/slice | solution.py:385
  18.0 0.0 copy-start.1
  18.0 0.0 copy-start.2
  18.0 0.0 copy-start.4
  18.0 0.0 copy-start.5
  18.0 0.0 copy-start.6
  18.0 4.1 %collective-permute-start.3 = (f32[128,1280]{1,0:T(8,128)}, f32[128,1280]{1,0:T(8,128)S(1)}, u32[]{:S(2)}, u32[]{:S(2)}) collective-permute-start(f32[128,1280]{1,0:T(8,128)} %get-tuple-element.31), channel_id=1, source_target_pairs={{32,0},{64,32},{96,64},{33,1},{65,33},{97,65},{34,2},{66,34},{98,6... | collective-permute-start | bytes 1966088 | tf_op jit(solution)/shard_map/ppermute | solution.py:385
  22.2 5.1 %collective-permute-start.2 = (f32[128,1280]{1,0:T(8,128)S(1)}, f32[128,1280]{1,0:T(8,128)S(1)}, u32[]{:S(2)}, u32[]{:S(2)}) collective-permute-start(f32[128,1280]{1,0:T(8,128)S(1)} %get-tuple-element.32), channel_id=1, source_target_pairs={{0,32},{32,64},{64,96},{1,33},{33,65},{65,97},{2,34},{34,66},{66,9... | collective-permute-start | bytes 1966088 | tf_op jit(solution)/shard_map/ppermute | solution.py:384
  27.3 0.1 pad_add_fusion.lat
  27.4 0.1 multiply_multiply_fusion
  27.4 0.0 copy-done.3
  27.5 0.1 broadcast_in_dim.2.invb
  27.6 17.5 %inner.1 = (f32[8,256,128]{2,1,0:T(8,128)S(1)}, f32[4,6,8,8,128]{4,3,2,1,0:T(8,128)S(1)}) custom-call(s32[8,8]{1,0:T(8,128)S(1)} %copy-done.3, f32[8,8]{1,0:T(8,128)S(1)} %convert_divide_fusion.inv_lags, f32[256,1024]{1,0:T(8,128)S(1)} %copy-done, f32[256,128]{1,0:T(8,128)S(1)} %collective-permute-done.west, f32[256,128]{1,0:T(8,128)S(1)} %collective-permute-done.1.east, ...), custom_call_target="tpu_custom_call" | custom-call | flops 400000000 | bytes 30000000 | tf_op jit(solution)/shard_map/inner/pallas_call | solution.py:192
  45.1 0.0 collective-permute-done.3.south
  45.1 0.0 collective-permute-done.2.north
  45.1 0.0 copy-done.1
  45.1 0.0 copy-done.2
  45.2 0.0 copy-done.4
  45.2 0.0 copy-done.5
  45.2 0.0 copy-done.6
  45.2 17.7 %outer.1 = (f32[256,1024]{1,0:T(8,128)}, f32[128,1408]{1,0:T(8,128)S(1)}) custom-call(s32[8,8]{1,0:T(8,128)S(1)} %copy-done.3, f32[8,8]{1,0:T(8,128)S(1)} %convert_divide_fusion.inv_lags, s32[1,128]{1,0:T(1,128)S(1)} %copy-done.6, s32[2]{0:T(128)S(1)} %pad_add_fusion.lat, f32[256,1024]{1,0:T(8,128)S(1)} %copy-done, ...), custom_call_target="tpu_custom_call" | custom-call | flops 400000000 | bytes 20000000 | tf_op jit(solution)/shard_map/outer/pallas_call | solution.py:303
  62.9 0.7 copy.8
  63.6 17.6 %all_to_all.11 = f32[128,1,1408]{2,1,0:T(1,128)S(1)} all-to-all(f32[128,1,1408]{2,1,0:T(1,128)S(1)} %copy.8), channel_id=1, replica_groups=mesh['lat'=4,'lon'=32] {'lat','lon'}, dimensions={0} | all-to-all | bytes 1441792 | tf_op jit(solution)/shard_map/all_to_all | solution.py:399
  81.3 3.4 %cells.1 = (f32[8,512]{1,0:T(8,128)}, f32[1,512]{1,0:T(1,128)}) custom-call(f32[128,1408]{1,0:T(8,128)S(1)} %bitcast.9), custom_call_target="tpu_custom_call" | custom-call | tf_op jit(solution)/shard_map/cells/pallas_call | solution.py:358
  (5 shorter events, 0.1 us)
Async XLA Ops:
  0.6 16.3 %copy-start = (f32[256,1024]{1,0:T(8,128)S(1)}, f32[256,1024]{1,0:T(8,128)}, u32[]{:S(2)}) copy-start(f32[256,1024]{1,0:T(8,128)} %own.3) | copy-start | bytes 3145732
  1.7 10.7 %collective-permute-start.1 = (f32[256,128]{1,0:T(8,128)S(1)}, f32[256,128]{1,0:T(8,128)S(1)}, u32[]{:S(2)}, u32[]{:S(2)}) collective-permute-start(f32[256,128]{1,0:T(8,128)S(1)} %get-tuple-element.33), channel_id=1, source_target_pairs={{1,0},{2,1},{3,2},{4,3},{5,4},{6,5},{7,6},{8,7},{9,8},{10,9},{11,1... | collective-permute-start | bytes 393224 | tf_op jit(solution)/shard_map/ppermute | solution.py:377
  8.9 8.0 %collective-permute-start = (f32[256,128]{1,0:T(8,128)S(1)}, f32[256,128]{1,0:T(8,128)S(1)}, u32[]{:S(2)}, u32[]{:S(2)}) collective-permute-start(f32[256,128]{1,0:T(8,128)S(1)} %get-tuple-element.34), channel_id=1, source_target_pairs={{0,1},{1,2},{2,3},{3,4},{4,5},{5,6},{6,7},{7,8},{8,9},{9,10},{10,1... | collective-permute-start | bytes 393224 | tf_op jit(solution)/shard_map/ppermute | solution.py:376
  17.1 10.4 %copy-start.3 = (s32[8,8]{1,0:T(8,128)S(1)}, s32[8,8]{1,0:T(8,128)}, u32[]{:S(2)}) copy-start(s32[8,8]{1,0:T(8,128)} %lags.3) | copy-start | bytes 772
  18.0 27.1 %copy-start.1 = (f32[2,128,128]{2,1,0:T(8,128)S(1)}, f32[2,128,128]{2,1,0:T(8,128)}, u32[]{:S(2)}) copy-start(f32[2,128,128]{2,1,0:T(8,128)} %get-tuple-element.26.meta) | copy-start | bytes 393220
  18.0 27.2 %copy-start.2 = (s32[96,128]{1,0:T(8,128)S(1)}, s32[96,128]{1,0:T(8,128)}, u32[]{:S(2)}) copy-start(s32[96,128]{1,0:T(8,128)} %get-tuple-element.25.index) | copy-start | bytes 147460
  18.0 27.2 %copy-start.4 = (s32[4096,1]{0,1:T(1,128)S(1)}, s32[4096,1]{0,1:T(1,128)}, u32[]{:S(2)}) copy-start(s32[4096,1]{0,1:T(1,128)} %param.7) | copy-start | bytes 49156
  18.0 27.2 %copy-start.5 = (s32[4096]{0:T(1024)S(1)}, s32[4096]{0:T(1024)}, u32[]{:S(2)}) copy-start(s32[4096]{0:T(1024)} %param.9) | copy-start | bytes 49156
  18.0 27.2 %copy-start.6 = (s32[1,128]{1,0:T(1,128)S(1)}, s32[1,128]{1,0:T(1,128)}, u32[]{:S(2)}) copy-start(s32[1,128]{1,0:T(1,128)} %get-tuple-element.20.starts) | copy-start | bytes 1540
  18.0 27.1 %collective-permute-start.3 = (f32[128,1280]{1,0:T(8,128)}, f32[128,1280]{1,0:T(8,128)S(1)}, u32[]{:S(2)}, u32[]{:S(2)}) collective-permute-start(f32[128,1280]{1,0:T(8,128)} %get-tuple-element.31), channel_id=1, source_target_pairs={{32,0},{64,32},{96,64},{33,1},{65,33},{97,65},{34,2},{66,34},{98,6... | collective-permute-start | bytes 1966088 | tf_op jit(solution)/shard_map/ppermute | solution.py:385
  22.2 23.0 %collective-permute-start.2 = (f32[128,1280]{1,0:T(8,128)S(1)}, f32[128,1280]{1,0:T(8,128)S(1)}, u32[]{:S(2)}, u32[]{:S(2)}) collective-permute-start(f32[128,1280]{1,0:T(8,128)S(1)} %get-tuple-element.32), channel_id=1, source_target_pairs={{0,32},{32,64},{64,96},{1,33},{33,65},{65,97},{2,34},{34,66},{66,9... | collective-permute-start | bytes 1966088 | tf_op jit(solution)/shard_map/ppermute | solution.py:384
where the time goes:
time: 85 us; the launch traced here: 84.7 us
  Pallas kernels  42.1 us (50%)
  blocking collectives  17.6 us (21%)
  starting transfers between devices  16.4 us (19%)
  waiting for transfers between devices  4.53 us (5%)
  local copies, waits for them, and re-layouts  3.04 us (4%)
    pallas_call x1, Pallas kernels, outer(): pl.pallas_call(outer_kernel, name='outer', out_shape=(jax.ShapeDtypeStruc...  17.7 us
    all_to_all x1, blocking collectives, shards(): lax.all_to_all(packed, ('lat', 'lon'), split_axis=0, concat_axis=0, tiled...  17.6 us
    pallas_call x1, Pallas kernels, inner(): pl.pallas_call(inner_kernel, name='inner', out_shape=(jax.ShapeDtypeStruc...  17.5 us
    ppermute x1, starting transfers between devices, shards(): east = lax.ppermute(own[:, :W], 'lon', east_pairs)  7.18 us
    ppermute x1, starting transfers between devices, shards(): north = lax.ppermute(wide[rows - W:], 'lat', down)  5.11 us
    ppermute x1, waiting for transfers between devices, shards(): lax.ppermute(own[:, width - W:], 'lon', [(j, i) for i, j in east_pairs])  4.52 us
    ppermute x1, starting transfers between devices, shards(): south = lax.ppermute(wide[:W], 'lat', [(j, i) for i, j in down])  4.14 us
    pallas_call x1, Pallas kernels, route(): pl.pallas_call(route_kernel, name='route', out_shape=(jax.ShapeDtypeStruc...  3.51 us
  transfers between devices with their start and end apart: 4, of which 1 were waited for; matrix products, arithmetic and copies ran while one was open for 0% of the time, Pallas kernels for 25%

commit v1 on v0

--- a/solution.py
+++ b/solution.py
@@ -99,61 +99,114 @@
     )(owner, slot, weight)
 
 
-def turned(z, r):
-    if z is None:
-        return (None, r)
-    x, y = z
-    if x is None:
-        return (1.0 - y * r, y + r)
-    return (x - y * r, y + x * r)
-
-
-def sample(lags, inv_lags, invb, H, h0, it, rays, S_ref, svf_in, svf_out):
+def quad(r):
+    x0, y0 = 1.0 - r[0] * r[1], r[0] + r[1]
+    x1, y1 = 1.0 - r[2] * r[3], r[2] + r[3]
+    return angle(x0 * x1 - y0 * y1, x0 * y1 + x1 * y0)
+
+
+class Ray:
+    def __init__(self, azimuth, step, near, far, inv_base, opening, put):
+        self.azimuth, self.step, self.near, self.far = azimuth, step, near, far
+        self.inv_base, self.opening, self.put = inv_base, opening, put
+
+
+def plane_rays(H, it, h0, rays, inv_base, V_old, V, S_ref):
     lane = iota((8, 128), 1)
     rc = lax.shift_right_logical(it, 1)
-    r0 = rc * 64 + lax.bitwise_and(it, 1) * 4
+    p0 = lax.bitwise_and(it, 1) * 4
+    block = pl.multiple_of(rc * 8, 8)
+    made = []
     for f, (a, sy, sx) in enumerate(rays):
-        flat = isinstance(sy, int) and sy == 0
-        z = [None] * 8
         off = 1 if sx >= 0 else 0
         count = 8 if sx == 0 else 9
-        for p in range(4):
-            here = r0 + p
-            t = [H[1 + j, pl.ds(h0 + here, 8, stride=8), :] for j in range(8)]
-            best = [None] * 8
-            if flat:
-                far = [H[off + j, pl.ds(h0 + here, 8, stride=8), :] for j in range(count)]
-            for k in range(KS):
-                s = lags[a, k]
-                il = inv_lags[a, k]
-                if not flat:
-                    row = h0 + here + sy * s
-                    far = [H[off + j, pl.ds(row, 8, stride=8), :] for j in range(count)]
-                if sx == 0:
-                    got = far
-                else:
-                    amount = 128 - s if sx == 1 else lax.bitwise_and(s, 127)
-                    keep = lane < (amount if sx == 1 else s)
-                    rolled = [pltpu.roll(v, amount, 1) for v in far]
-                    got = [jnp.where(keep, rolled[j], rolled[j + 1]) for j in range(8)]
+
+        def near(p):
+            rows = pl.ds(pl.multiple_of(h0 // 8 + rc * 8, 8), 8)
+            return [H[1 + j, p0 + p, rows, :] for j in range(8)]
+
+        def far(p, s, sy=sy, sx=sx, off=off, count=count):
+            y = h0 + rc * 64 + p0 + p + sy * s
+            plane, i0 = lax.bitwise_and(y, 7), lax.shift_right_logical(y, 3)
+            tiles = [H[off + j, plane, pl.ds(i0, 8), :] for j in range(count)]
+            if sx == 0:
+                return tiles
+            amount = 128 - s if sx == 1 else lax.bitwise_and(s, 127)
+            keep = lane < (amount if sx == 1 else s)
+            rolled = [pltpu.roll(v, amount, 1) for v in tiles]
+            return [jnp.where(keep, rolled[j], rolled[j + 1]) for j in range(8)]
+
+        def base(p, sx=sx):
+            return 1.0 / pixel_size if sx == 0 else inv_base[p0 + p, pl.ds(block, 8), :]
+
+        def opening(p, j, v, f=f):
+            old = V_old if f == 0 else V
+            at = (j, p0 + p, pl.ds(block, 8))
+            V[at] = v if old is None else old[at] + v
+
+        def put(j, v, f=f):
+            S_ref[rc, f, j] += v
+
+        made.append(Ray(a, sy, near, far, base, opening, put))
+    return made
+
+
+def turned_rays(H, it, inv_row, V, S_ref):
+    rt = lax.shift_right_logical(it, 2)
+    half = lax.bitwise_and(lax.shift_right_logical(it, 1), 1)
+    p0 = lax.bitwise_and(it, 1) * 4
+    made = []
+    for f, (a, sx) in enumerate(((0, 1), (4, -1))):
+
+        def near(p):
+            return [H[rt, p0 + p, pl.ds(pl.multiple_of(16 + half * 64 + 8 * j, 8), 8), :] for j in range(8)]
+
+        def far(p, s, sx=sx):
+            x = 128 + half * 512 + p0 + p + sx * s
+            plane, i0 = lax.bitwise_and(x, 7), lax.shift_right_logical(x, 3)
+            return [H[rt, plane, pl.ds(i0 + 8 * j, 8), :] for j in range(8)]
+
+        def base(p):
+            return jnp.broadcast_to(inv_row[pl.ds(rt, 1), :], (8, 128))
+
+        def rows(j):
+            return pl.ds(pl.multiple_of(half * 64 + 8 * j, 8), 8)
+
+        def opening(p, j, v, f=f):
+            at = (rt, p0 + p, rows(j))
+            V[at] = v if f == 0 else V[at] + v
+
+        def put(j, v, f=f):
+            S_ref[rt, f, rows(j), :] += v
+
+        made.append(Ray(a, sx, near, far, base, opening, put))
+    return made
+
+
+def march(lags, inv_lags, group, rise):
+    for p in range(4):
+        t = [ray.near(p) for ray in group]
+        best = [[None] * 8 for ray in group]
+        for k in range(KS):
+            for i, ray in enumerate(group):
+                inv_lag = inv_lags[ray.azimuth, k]
+                got = ray.far(p, lags[ray.azimuth, k])
                 for j in range(8):
-                    v = (got[j] - t[j]) * il
-                    best[j] = v if k == 0 else jnp.maximum(best[j], v)
-            ib = 1.0 / pixel_size if sx == 0 else invb[1 if flat else 0, pl.ds(here, 8, stride=8), :]
+                    v = (got[j] - t[i][j]) * inv_lag
+                    best[i][j] = v if k == 0 else jnp.maximum(best[i][j], v)
+        for i, ray in enumerate(group):
+            ib = ray.inv_base(p)
             for j in range(8):
-                rise = jnp.minimum(jnp.maximum(best[j] * ib, 0.0), 1e8)
-                z[j] = turned(z[j], rise)
-                opening = recip(1.0 + rise * rise)
-                if f == 0 and svf_in is not None:
-                    opening = opening + svf_in[j, pl.ds(here, 8, stride=8), :]
-                if f > 0:
-                    opening = opening + svf_out[j, pl.ds(here, 8, stride=8), :]
-                svf_out[j, pl.ds(here, 8, stride=8), :] = opening
+                rise[i, p, j] = jnp.minimum(jnp.maximum(best[i][j] * ib, 0.0), 1e8)
+
+
+def finish(group, rise):
+    for i, ray in enumerate(group):
         for j in range(8):
-            S_ref[rc, f, j] += angle(*z[j])
-    for j in range(8):
-        v = [svf_out[j, pl.ds(r0 + p, 8, stride=8), :] for p in range(4)]
-        S_ref[rc, len(rays), j] += (v[0] + v[1]) + (v[2] + v[3])
+            r = [rise[i, p, j] for p in range(4)]
+            for p in range(4):
+                ray.opening(p, j, recip(1.0 + r[p] * r[p]))
+            ray.put(j, quad(r))
 
 
 def slanted(southward):
@@ -173,76 +226,140 @@
     return pl.ds(j * 128, 128)
 
 
-def inner_kernel(lags, inv_lags, own, west, east, invb, V_ref, S_ref, H, sems):
+def inner_kernel(
+    lags, inv_lags, own, west, east, inv_base, inv_row, V_ref, S_ref, pooled_ref, Hn, H, Tn, T, VT, ST, X, Xn, rise, sems
+):
     copies(
-        [(own.at[:, cols(j)], H.at[1 + j]) for j in range(8)] + [(west, H.at[0]), (east, H.at[9])], sems
+        [(own.at[:, cols(j)], Hn.at[1 + j]) for j in range(8)] + [(west, Hn.at[0]), (east, Hn.at[9])], sems
     )
-
+    for c in range(10):
+        for p in range(8):
+            H[c, p] = Hn[c, pl.ds(p, 32, stride=8), :]
+        for rt in range(2):
+            Tn[rt, c * 128 : (c + 1) * 128, :] = Hn[c, rt * 128 : (rt + 1) * 128, :].T
+    for rt in range(2):
+        for p in range(8):
+            T[rt, p] = Tn[rt, pl.ds(p, 160, stride=8), :]
     S_ref[...] = jnp.zeros(S_ref.shape, F32)
+    ST[...] = jnp.zeros(ST.shape, F32)
 
     def step(it, carry):
-        rays = [(0, 0, 1), (4, 0, -1)] + slanted(it < 4)
-        sample(lags, inv_lags, invb, H, 0, it, rays, S_ref, None, V_ref)
+        left, up, right = plane_rays(H, it, 0, slanted(it < 4), inv_base, None, V_ref, S_ref)
+        along, against = turned_rays(T, it, inv_row, VT, ST)
+        groups = ((left, along), (right, against), (up,))
+        order = (0, 2, 1)
+        for n, g in enumerate(groups):
+            march(lags, inv_lags, g, rise.at[n])
+        for n in order:
+            finish(groups[n], rise.at[n])
         return carry
 
     lax.fori_loop(0, 8, step, 0)
+    pool = (iota((16, 128), 0) == lax.shift_right_logical(iota((16, 128), 1), 3)).astype(BF16)
+    for rt in range(2):
+        for f in range(2):
+            hi, lo = split2(ST[rt, f])
+            total = lax.dot_general(pool, hi, NT, preferred_element_type=F32)
+            pooled_ref[f, rt * 16 : rt * 16 + 16, :] = total + lax.dot_general(pool, lo, NT, preferred_element_type=F32)
+        for c in range(8):
+            for p in range(8):
+                X[rt, c, pl.ds(p, 16, stride=8), :] = VT[rt, p, c * 16 : (c + 1) * 16, :]
+    for rt in range(2):
+        for c in range(8):
+            Xn[rt, c] = X[rt, c].T
+    for rt in range(2):
+        for c in range(8):
+            for p in range(8):
+                V_ref[c, p, rt * 16 : rt * 16 + 16, :] += Xn[rt, c, pl.ds(p, 16, stride=8), :]
 
 
 def inner(*args):
     return pl.pallas_call(
         inner_kernel,
         name="inner",
-        out_shape=(jax.ShapeDtypeStruct((8, 256, 128), F32), jax.ShapeDtypeStruct((4, 6, 8, 8, 128), F32)),
-        in_specs=[SMEM] * 2 + [ANY] * 3 + [VMEM],
-        out_specs=[VMEM] * 2,
-        scratch_shapes=[pltpu.VMEM((10, 256, 128), F32), pltpu.SemaphoreType.DMA((10,))],
-        compiler_params=pltpu.CompilerParams(vmem_limit_bytes=24 * 1024 * 1024),
+        out_shape=(
+            jax.ShapeDtypeStruct((8, 8, 32, 128), F32),
+            jax.ShapeDtypeStruct((4, 3, 8, 8, 128), F32),
+            jax.ShapeDtypeStruct((2, NBR, 128), F32),
+        ),
+        in_specs=[SMEM] * 2 + [ANY] * 3 + [VMEM] * 2,
+        out_specs=[VMEM] * 3,
+        scratch_shapes=[
+            pltpu.VMEM((10, 256, 128), F32),
+            pltpu.VMEM((10, 8, 32, 128), F32),
+            pltpu.VMEM((2, 1280, 128), F32),
+            pltpu.VMEM((2, 8, 160, 128), F32),
+            pltpu.VMEM((2, 8, 128, 128), F32),
+            pltpu.VMEM((2, 2, 128, 128), F32),
+            pltpu.VMEM((2, 8, 128, 128), F32),
+            pltpu.VMEM((2, 8, 128, 128), F32),
+            pltpu.VMEM((3, 2, 4, 8, 8, 128), F32),
+            pltpu.SemaphoreType.DMA((10,)),
+        ],
+        compiler_params=pltpu.CompilerParams(vmem_limit_bytes=32 * 1024 * 1024),
         cost_estimate=pl.CostEstimate(flops=int(4e8), bytes_accessed=30000000, transcendentals=0),
     )(*args)
 
 
 def outer_kernel(
-    lags, inv_lags, starts, lat, own, north, south, west, east, invb, V_in, S_in, weight, owner, index, meta,
-    svf_ref, out_ref, H, S, V, R, Z, Y, O, F, acc, sems,
+    lags, inv_lags, starts, lat, own, north, south, west, east, inv_base, V_in, S_in, pooled, weight, owner, index, meta,
+    svf_ref, out_ref, Hn, H, S, V, Vn, R, Z, Y, O, acc, rise, sems,
 ):
-    pairs = [(own.at[:, cols(j)], H.at[1 + j, pl.ds(128, 256)]) for j in range(8)]
-    pairs += [(west, H.at[0, pl.ds(128, 256)]), (east, H.at[9, pl.ds(128, 256)])]
-    pairs += [(north.at[:, cols(j)], H.at[j, pl.ds(0, 128)]) for j in range(10)]
-    pairs += [(south.at[:, cols(j)], H.at[j, pl.ds(384, 128)]) for j in range(10)]
+    pairs = [(own.at[:, cols(j)], Hn.at[1 + j, pl.ds(128, 256)]) for j in range(8)]
+    pairs += [(west, Hn.at[0, pl.ds(128, 256)]), (east, Hn.at[9, pl.ds(128, 256)])]
+    pairs += [(north.at[:, cols(j)], Hn.at[j, pl.ds(0, 128)]) for j in range(10)]
+    pairs += [(south.at[:, cols(j)], Hn.at[j, pl.ds(384, 128)]) for j in range(10)]
     copies(pairs, sems)
 
     @pl.when(lat[0] == 0)
     def _():
         for c in range(10):
-            H[c, 0:128, :] = jnp.broadcast_to(H[c, 128:129, :], (128, 128))
+            Hn[c, 0:128, :] = jnp.broadcast_to(Hn[c, 128:129, :], (128, 128))
 
     @pl.when(lat[0] == lat[1] - 1)
     def _():
         for c in range(10):
-            H[c, 384:512, :] = jnp.broadcast_to(H[c, 383:384, :], (128, 128))
-
+            Hn[c, 384:512, :] = jnp.broadcast_to(Hn[c, 383:384, :], (128, 128))
+
+    for c in range(10):
+        for p in range(8):
+            H[c, p] = Hn[c, pl.ds(p, 64, stride=8), :]
     S[...] = jnp.zeros(S.shape, F32)
 
     def step(it, carry):
-        sample(lags, inv_lags, invb, H, 128, it, slanted(it >= 4), S, V_in, V)
+        left, up, right = plane_rays(H, it, 128, slanted(it >= 4), inv_base, V_in, V, S)
+        groups = ((left, up), (right,))
+        for n, g in enumerate(groups):
+            march(lags, inv_lags, g, rise.at[n])
+        for n, g in enumerate(groups):
+            finish(g, rise.at[n])
         return carry
 
     lax.fori_loop(0, 8, step, 0)
+    svf_rows = []
     for j in range(8):
-        svf_ref[:, j * 128 : (j + 1) * 128] = V[j] * (1.0 / AZ)
-
-    total = jnp.zeros((288, 128), F32)
+        rows = V[j, 0]
+        for p in range(8):
+            Vn[j, pl.ds(p, 32, stride=8), :] = V[j, p] * (1.0 / AZ)
+            rows = rows if p == 0 else rows + V[j, p]
+        svf_rows.append(rows)
+    for j in range(8):
+        svf_ref[:, j * 128 : (j + 1) * 128] = Vn[j]
+
+    total = jnp.zeros((224, 128), F32)
     for j in range(8):
         pool = (iota((128, 128), 1) == j * 16 + lax.shift_right_logical(iota((128, 128), 0), 3)).astype(BF16)
         field = []
         for rc in range(4):
-            here, there = ((S_in, 2), (S, 0)) if rc < 2 else ((S, 0), (S_in, 2))
-            where = [(S_in, 0), (here[0], here[1] + 2), (here[0], here[1] + 1), (here[0], here[1])]
-            where += [(S_in, 1), (there[0], there[1]), (there[0], there[1] + 1), (there[0], there[1] + 2), (S, 3)]
-            field += [ref[rc, f, j] for ref, f in where]
+            south, north_ = (S_in, S) if rc < 2 else (S, S_in)
+            field += [south[rc, 2, j], south[rc, 1, j], south[rc, 0, j], north_[rc, 0, j], north_[rc, 1, j], north_[rc, 2, j]]
+            field.append(svf_rows[j][rc * 8 : rc * 8 + 8, :])
         hi, lo = split2(jnp.concatenate(field, axis=0))
         total = total + jnp.dot(hi, pool, preferred_element_type=F32) + jnp.dot(lo, pool, preferred_element_type=F32)
-    R[...] = total
+    for rc in range(4):
+        part = [total[rc * 56 + 8 * i : rc * 56 + 8 * i + 8] for i in range(7)]
+        flat = [pooled[f, rc * 8 : rc * 8 + 8, :] for f in range(2)]
+        R[rc * 72 : rc * 72 + 72, :] = jnp.concatenate([flat[0]] + part[:3] + [flat[1]] + part[3:], axis=0)
     lane = iota((8, 128), 1)
     scale = 1.0 / 4096.0
     for rc in range(4):
@@ -277,7 +394,9 @@
     for t in range(NBR):
         Z[t] = acc[t * 16 : t * 16 + 8, :] + acc[t * 16 + 8 : t * 16 + 16, :]
     Z[32] = jnp.zeros((8, 128), F32)
-    out_ref[:, 8 * 128 : 9 * 128] = acc[512:640, :] + acc[640:768, :]
+    out_ref[pl.ds(8, N_DEV, stride=11), :] = acc[512:640, :] + acc[640:768, :]
+    out_ref[pl.ds(9, N_DEV, stride=11), :] = meta[0]
+    out_ref[pl.ds(10, N_DEV, stride=11), :] = meta[1]
 
     def expand(o, carry):
         st = starts[0, o]
@@ -289,33 +408,31 @@
         keep = lane < q
         a = pltpu.roll(Z[tile], amount, 1)
         b = pltpu.roll(Z[after], amount, 1)
-        F[pl.ds(o, 8, stride=N_DEV), :] = jnp.where(keep, a, b)
+        out_ref[pl.ds(o * 11, 8), :] = jnp.where(keep, a, b)
         return carry
 
     lax.fori_loop(0, N_DEV, expand, 0, unroll=8)
-    for f in range(8):
-        out_ref[:, f * 128 : (f + 1) * 128] = F[f * N_DEV : (f + 1) * N_DEV, :]
-    out_ref[:, 9 * 128 : 10 * 128] = meta[0]
-    out_ref[:, 10 * 128 : 11 * 128] = meta[1]
 
 
 def outer(*args):
     return pl.pallas_call(
         outer_kernel,
         name="outer",
-        out_shape=(jax.ShapeDtypeStruct((256, 1024), F32), jax.ShapeDtypeStruct((N_DEV, 11 * 128), F32)),
-        in_specs=[SMEM] * 4 + [ANY] * 5 + [VMEM] * 7,
+        out_shape=(jax.ShapeDtypeStruct((256, 1024), F32), jax.ShapeDtypeStruct((N_DEV * 11, 128), F32)),
+        in_specs=[SMEM] * 4 + [ANY] * 5 + [VMEM] * 8,
         out_specs=[VMEM] * 2,
         scratch_shapes=[
             pltpu.VMEM((10, 512, 128), F32),
-            pltpu.VMEM((4, 4, 8, 8, 128), F32),
+            pltpu.VMEM((10, 8, 64, 128), F32),
+            pltpu.VMEM((4, 3, 8, 8, 128), F32),
+            pltpu.VMEM((8, 8, 32, 128), F32),
             pltpu.VMEM((8, 256, 128), F32),
             pltpu.VMEM((288, 128), F32),
             pltpu.VMEM((33, 8, 128), F32),
             pltpu.VMEM((32, 8, 128), F32),
             pltpu.VMEM((32, 128), F32),
-            pltpu.VMEM((8 * N_DEV, 128), F32),
             pltpu.VMEM((768, 128), F32),
+            pltpu.VMEM((2, 2, 4, 8, 8, 128), F32),
             pltpu.SemaphoreType.DMA((30,)),
         ],
         compiler_params=pltpu.CompilerParams(vmem_limit_bytes=32 * 1024 * 1024),
@@ -323,35 +440,29 @@
     )(*args)
 
 
-def cells_kernel(got_ref, horizon_ref, svf_ref, G):
-    for f in range(9):
-        G[pl.ds(f, N_DEV, stride=16), :] = got_ref[:, f * 128 : (f + 1) * 128]
-    cell = got_ref[:, 9 * 128 : 10 * 128].astype(jnp.int32) - 1
-    G[pl.ds(9, N_DEV, stride=16), :] = lax.shift_right_arithmetic(cell, 7).astype(F32)
-    G[pl.ds(10, N_DEV, stride=16), :] = got_ref[:, 10 * 128 : 11 * 128]
-    G[pl.ds(11, N_DEV, stride=16), :] = lax.bitwise_and(cell, 127).astype(F32)
-    for f in range(12, 16):
-        G[pl.ds(f, N_DEV, stride=16), :] = jnp.zeros((N_DEV, 128), F32)
+def cells_kernel(got_ref, horizon_ref, svf_ref):
     low = iota((128, 512), 0).astype(F32).astype(BF16)
 
     def accumulate(t, acc):
-        base = pl.multiple_of(t * 64, 64)
-        v = jnp.concatenate([G[pl.ds(base + 16 * i, 16), :] for i in range(4)], axis=1)
-        hi, lo = split2(v)
-        high = jnp.broadcast_to(v[9:10, :], (16, 512)).astype(BF16)
+        first = jnp.concatenate([got_ref[pl.ds(t * 44 + 11 * i, 8), :] for i in range(4)], axis=1)
+        second = jnp.concatenate([got_ref[pl.ds(t * 44 + 11 * i + 3, 8), :] for i in range(4)], axis=1)
+        hi, lo = split2(jnp.concatenate([first, second], axis=0))
+        cell = second[6:7, :] - 1.0
+        upper = jnp.floor(cell * (1.0 / 128.0))
+        high = jnp.broadcast_to(upper, (16, 512)).astype(BF16)
         zero = jnp.zeros((16, 512), BF16)
         left = []
         for h in range(4):
             mine = high == BF16(h)
             left += [jnp.where(mine, hi, zero), jnp.where(mine, lo, zero)]
-        hot = (low == jnp.broadcast_to(v[11:12, :], (128, 512)).astype(BF16)).astype(BF16)
+        hot = (low == jnp.broadcast_to(cell - 128.0 * upper, (128, 512)).astype(BF16)).astype(BF16)
         return acc + lax.dot_general(jnp.concatenate(left, axis=0), hot, NT, preferred_element_type=F32)
 
     acc = lax.fori_loop(0, N_DEV // 4, accumulate, jnp.zeros((128, 128), F32), unroll=8)
     sums = jnp.concatenate([acc[h * 32 : h * 32 + 16] + acc[h * 32 + 16 : h * 32 + 32] for h in range(4)], axis=1)
-    area = jnp.maximum(sums[10:11, :] * (1.0 / 64.0), 1.0)
+    area = jnp.maximum(sums[15:16, :] * (1.0 / 64.0), 1.0)
     horizon_ref[...] = sums[0:8] / area
-    svf_ref[...] = sums[8:9] / area
+    svf_ref[...] = sums[13:14] / area
 
 
 def cells(got):
@@ -361,7 +472,6 @@
         out_shape=(jax.ShapeDtypeStruct((AZ, CELLS_DEV), F32), jax.ShapeDtypeStruct((1, CELLS_DEV), F32)),
         in_specs=[VMEM],
         out_specs=[VMEM] * 2,
-        scratch_shapes=[pltpu.VMEM((16 * N_DEV, 128), F32)],
         compiler_params=pltpu.CompilerParams(vmem_limit_bytes=24 * 1024 * 1024),
     )(got)
 
@@ -388,15 +498,19 @@
     latitude = 47.0 - (rows_global + 0.5) / 1200.0
     coslat = jnp.cos(latitude * jnp.pi / 180.0)
     across = (pixel_size * coslat) ** 2
-    inv_base = 1.0 / jnp.sqrt(jnp.stack([pixel_size**2 + across, across]))
-    inv_base = jnp.broadcast_to(inv_base[:, :, None], (2, rows, 128))
+    inv_row = (1.0 / jnp.sqrt(across)).reshape(2, 128)
+    inv_base = 1.0 / jnp.sqrt(pixel_size**2 + across)
+    inv_base = jnp.broadcast_to(inv_base.reshape(32, 8).T[:, :, None], (8, 32, 128))
     lat = jnp.stack([lax.axis_index("lat").astype(jnp.int32), jnp.int32(n_lat)])
     inv_lags = 1.0 / azimuth_lag_tallies.astype(F32)
-    part, sums = inner(azimuth_lag_tallies, inv_lags, own, west, east, inv_base)
+    part, sums, pooled = inner(azimuth_lag_tallies, inv_lags, own, west, east, inv_base, inv_row)
     fine_svf, packed = outer(
-        azimuth_lag_tallies, inv_lags, start, lat, own, north, south, west, east, inv_base, part, sums, weight, owner, index, meta
+        azimuth_lag_tallies, inv_lags, start, lat, own, north, south, west, east, inv_base, part, sums, pooled,
+        weight, owner, index, meta,
     )
+    packed = packed.reshape(N_DEV, 1, 11 * 128)
     got = lax.all_to_all(packed, ("lat", "lon"), split_axis=0, concat_axis=0, tiled=True)
+    got = got.reshape(N_DEV * 11, 128)
     cell_horizon, cell_svf = cells(got)
     return fine_svf, cell_horizon, cell_svf.reshape(CELLS_DEV)
 

time: 85 us -> 75.8 us (0.89)
  Pallas kernels: 42.1 us -> 33.8 us
    pallas_call x1, Pallas kernels: 17.5 us -> 12.6 us  [inner(): pl.pallas_call(inner_kernel, name='inner', out_shape=(jax.ShapeDtypeStruc...]
    pallas_call x1, Pallas kernels: 17.7 us -> 14.7 us  [outer(): pl.pallas_call(outer_kernel, name='outer', out_shape=(jax.ShapeDtypeStruc...]
  transfers between devices with their start and end apart: 4 -> 4, of which waited for: 1 -> 1; matrix products, arithmetic and copies ran while one was open for 0% -> 0% of each run, Pallas kernels for 25% -> 21%
where the time goes in v1:
time: 75.8 us; the launch traced here: 75.5 us
  Pallas kernels  33.8 us (45%)
  blocking collectives  17.6 us (23%)
  starting transfers between devices  16.4 us (22%)
  waiting for transfers between devices  4.53 us (6%)
  local copies, waits for them, and re-layouts  2.21 us (3%)
  between operations  0.82 us (1%)
    all_to_all x1, blocking collectives, shards(): lax.all_to_all(packed, ('lat', 'lon'), split_axis=0, concat_axis=0, tiled...  17.6 us
    pallas_call x1, Pallas kernels, outer(): pl.pallas_call(outer_kernel, name='outer', out_shape=(jax.ShapeDtypeStruc...  14.7 us
    pallas_call x1, Pallas kernels, inner(): pl.pallas_call(inner_kernel, name='inner', out_shape=(jax.ShapeDtypeStruc...  12.6 us
    ppermute x1, starting transfers between devices, shards(): east = lax.ppermute(own[:, :W], 'lon', east_pairs)  7.18 us
    ppermute x1, starting transfers between devices, shards(): north = lax.ppermute(wide[rows - W:], 'lat', down)  5.11 us
    ppermute x1, waiting for transfers between devices, shards(): lax.ppermute(own[:, width - W:], 'lon', [(j, i) for i, j in east_pairs])  4.52 us
    ppermute x1, starting transfers between devices, shards(): south = lax.ppermute(wide[:W], 'lat', [(j, i) for i, j in down])  4.14 us
    pallas_call x1, Pallas kernels, route(): pl.pallas_call(route_kernel, name='route', out_shape=(jax.ShapeDtypeStruc...  3.51 us
  transfers between devices with their start and end apart: 4, of which 1 were waited for; matrix products, arithmetic and copies ran while one was open for 0% of the time, Pallas kernels for 21%

profile of v1, /device:TPU:1, one launch (start us, length us, event | category | flops | bytes accessed | tf_op | source)
XLA Modules:
  0.0 75.5 jit_solution(13587880826621290766)
XLA Ops:
  0.6 0.0 copy-start
  0.6 1.1 %fusion.1 = (f32[256,128]{1,0:T(8,128)S(1)}, f32[256,128]{1,0:T(8,128)S(1)}) fusion(f32[256,1024]{1,0:T(8,128)} %own.3), kind=kLoop, calls=%fused_computation.8 | loop fusion | bytes 524288 | tf_op jit(solution)/shard_map/slice | solution.py:487
  1.7 7.2 %collective-permute-start.1 = (f32[256,128]{1,0:T(8,128)S(1)}, f32[256,128]{1,0:T(8,128)S(1)}, u32[]{:S(2)}, u32[]{:S(2)}) collective-permute-start(f32[256,128]{1,0:T(8,128)S(1)} %get-tuple-element.35), channel_id=1, source_target_pairs={{1,0},{2,1},{3,2},{4,3},{5,4},{6,5},{7,6},{8,7},{9,8},{10,9},{11,1... | collective-permute-start | bytes 393224 | tf_op jit(solution)/shard_map/ppermute | solution.py:487
  8.9 0.0 collective-permute-start
  8.9 3.5 %route.1 = (s32[1,128]{1,0:T(1,128)}, s32[96,128]{1,0:T(8,128)}, f32[2,128,128]{2,1,0:T(8,128)}) custom-call(s32[32,128]{1,0:T(8,128)} %bitcast.9, s32[32,128]{1,0:T(8,128)} %bitcast.13, s32[32,128]{1,0:T(8,128)} %bitcast.11), custom_call_target="tpu_custom_call" | custom-call | flops 400000000 | bytes 200000 | tf_op jit(solution)/shard_map/route/pallas_call | solution.py:87
  12.4 0.0 collective-permute-done.1.east
  12.4 4.5 %collective-permute-done.west = f32[256,128]{1,0:T(8,128)S(1)} collective-permute-done((f32[256,128]{1,0:T(8,128)S(1)}, f32[256,128]{1,0:T(8,128)S(1)}, u32[]{:S(2)}, u32[]{:S(2)}) %collective-permute-start) | collective-permute-done | bytes 131104 | tf_op jit(solution)/shard_map/ppermute | solution.py:486
  17.0 0.0 copy-done
  17.0 0.1 constant_dynamic-update-slice_fusion.1
  17.1 0.0 copy-start.5
  17.1 0.9 %fusion = (f32[128,1280]{1,0:T(8,128)}, f32[128,1280]{1,0:T(8,128)S(1)}) fusion(f32[256,1280]{1,0:T(8,128)S(1)} %constant_dynamic-update-slice_fusion), kind=kLoop, calls=%fused_computation.7 | loop fusion | bytes 2621440 | tf_op jit(solution)/shard_map/slice | solution.py:495
  18.0 0.0 copy-start.1
  18.0 0.0 copy-start.2
  18.0 0.0 copy-start.3
  18.0 0.0 copy-start.4
  18.0 0.0 copy-start.6
  18.0 4.1 %collective-permute-start.3 = (f32[128,1280]{1,0:T(8,128)}, f32[128,1280]{1,0:T(8,128)S(1)}, u32[]{:S(2)}, u32[]{:S(2)}) collective-permute-start(f32[128,1280]{1,0:T(8,128)} %get-tuple-element.33), channel_id=1, source_target_pairs={{32,0},{64,32},{96,64},{33,1},{65,33},{97,65},{34,2},{66,34},{98,6... | collective-permute-start | bytes 1966088 | tf_op jit(solution)/shard_map/ppermute | solution.py:495
  22.2 5.1 %collective-permute-start.2 = (f32[128,1280]{1,0:T(8,128)S(1)}, f32[128,1280]{1,0:T(8,128)S(1)}, u32[]{:S(2)}, u32[]{:S(2)}) collective-permute-start(f32[128,1280]{1,0:T(8,128)S(1)} %get-tuple-element.34), channel_id=1, source_target_pairs={{0,32},{32,64},{64,96},{1,33},{33,65},{65,97},{2,34},{34,66},{66,9... | collective-permute-start | bytes 1966088 | tf_op jit(solution)/shard_map/ppermute | solution.py:494
  27.3 0.1 pad_add_fusion.lat
  27.4 0.1 multiply_rsqrt_fusion.inv_row
  27.4 0.1 add_rsqrt_fusion
  27.5 0.0 copy-done.5
  27.5 0.1 broadcast_in_dim.2.inv_base
  27.6 12.6 %inner.1 = (f32[8,8,32,128]{3,2,1,0:T(8,128)S(1)}, f32[4,3,8,8,128]{4,3,2,1,0:T(8,128)S(1)}, f32[2,32,128]{2,1,0:T(8,128)S(1)}) custom-call(s32[8,8]{1,0:T(8,128)S(1)} %copy-done.5, f32[8,8]{1,0:T(8,128)S(1)} %convert_divide_fusion.inv_lags, f32[256,1024]{1,0:T(8,128)S(1)} %copy-done, f32[256,128]{1,0:T(8,128)S(1)} %collective-permute-done.west, ...), custom_call_target="tpu_custom_call" | custom-call | flops 400000000 | bytes 30000000 | tf_op jit(solution)/shard_map/inner/pallas_call | solution.py:277
  40.2 0.0 collective-permute-done.3.south
  40.2 0.0 collective-permute-done.2.north
  40.2 0.0 copy-done.1
  40.3 0.0 copy-done.2
  40.3 0.0 copy-done.3
  40.3 0.0 copy-done.4
  40.3 0.0 copy-done.6
  40.3 14.7 %outer.1 = (f32[256,1024]{1,0:T(8,128)}, f32[1408,128]{1,0:T(8,128)S(1)}) custom-call(s32[8,8]{1,0:T(8,128)S(1)} %copy-done.5, f32[8,8]{1,0:T(8,128)S(1)} %convert_divide_fusion.inv_lags, s32[1,128]{1,0:T(1,128)S(1)} %copy-done.6, s32[2]{0:T(128)S(1)} %pad_add_fusion.lat, f32[256,1024]{1,0:T(8,128)S(1)} %copy-done, ...), custom_call_target="tpu_custom_call" | custom-call | flops 400000000 | bytes 20000000 | tf_op jit(solution)/shard_map/outer/pallas_call | solution.py:418
  55.0 17.6 %all_to_all.5 = f32[128,1,1408]{2,1,0:T(1,128)S(1)} all-to-all(f32[128,1,1408]{2,1,0:T(1,128)S(1)} %bitcast.8), channel_id=1, replica_groups=mesh['lat'=4,'lon'=32] {'lat','lon'}, dimensions={0} | all-to-all | bytes 1441792 | tf_op jit(solution)/shard_map/all_to_all | solution.py:512
  72.6 3.0 %cells.1 = (f32[8,512]{1,0:T(8,128)}, f32[1,512]{1,0:T(1,128)}) custom-call(f32[1408,128]{1,0:T(8,128)S(1)} %bitcast.7), custom_call_target="tpu_custom_call" | custom-call | tf_op jit(solution)/shard_map/cells/pallas_call | solution.py:469
  (3 shorter events, 0.0 us)
Async XLA Ops:
  0.6 16.3 %copy-start = (f32[256,1024]{1,0:T(8,128)S(1)}, f32[256,1024]{1,0:T(8,128)}, u32[]{:S(2)}) copy-start(f32[256,1024]{1,0:T(8,128)} %own.3) | copy-start | bytes 3145732
  1.7 10.7 %collective-permute-start.1 = (f32[256,128]{1,0:T(8,128)S(1)}, f32[256,128]{1,0:T(8,128)S(1)}, u32[]{:S(2)}, u32[]{:S(2)}) collective-permute-start(f32[256,128]{1,0:T(8,128)S(1)} %get-tuple-element.35), channel_id=1, source_target_pairs={{1,0},{2,1},{3,2},{4,3},{5,4},{6,5},{7,6},{8,7},{9,8},{10,9},{11,1... | collective-permute-start | bytes 393224 | tf_op jit(solution)/shard_map/ppermute | solution.py:487
  8.9 8.0 %collective-permute-start = (f32[256,128]{1,0:T(8,128)S(1)}, f32[256,128]{1,0:T(8,128)S(1)}, u32[]{:S(2)}, u32[]{:S(2)}) collective-permute-start(f32[256,128]{1,0:T(8,128)S(1)} %get-tuple-element.36), channel_id=1, source_target_pairs={{0,1},{1,2},{2,3},{3,4},{4,5},{5,6},{6,7},{7,8},{8,9},{9,10},{10,1... | collective-permute-start | bytes 393224 | tf_op jit(solution)/shard_map/ppermute | solution.py:486
  17.1 10.4 %copy-start.5 = (s32[8,8]{1,0:T(8,128)S(1)}, s32[8,8]{1,0:T(8,128)}, u32[]{:S(2)}) copy-start(s32[8,8]{1,0:T(8,128)} %lags.3) | copy-start | bytes 772
  18.0 22.3 %copy-start.1 = (f32[2,128,128]{2,1,0:T(8,128)S(1)}, f32[2,128,128]{2,1,0:T(8,128)}, u32[]{:S(2)}) copy-start(f32[2,128,128]{2,1,0:T(8,128)} %get-tuple-element.28.meta) | copy-start | bytes 393220
  18.0 22.3 %copy-start.2 = (s32[96,128]{1,0:T(8,128)S(1)}, s32[96,128]{1,0:T(8,128)}, u32[]{:S(2)}) copy-start(s32[96,128]{1,0:T(8,128)} %get-tuple-element.27.index) | copy-start | bytes 147460
  18.0 22.3 %copy-start.3 = (s32[4096,1]{0,1:T(1,128)S(1)}, s32[4096,1]{0,1:T(1,128)}, u32[]{:S(2)}) copy-start(s32[4096,1]{0,1:T(1,128)} %param.7) | copy-start | bytes 49156
  18.0 22.3 %copy-start.4 = (s32[4096]{0:T(1024)S(1)}, s32[4096]{0:T(1024)}, u32[]{:S(2)}) copy-start(s32[4096]{0:T(1024)} %param.9) | copy-start | bytes 49156
  18.0 22.3 %copy-start.6 = (s32[1,128]{1,0:T(1,128)S(1)}, s32[1,128]{1,0:T(1,128)}, u32[]{:S(2)}) copy-start(s32[1,128]{1,0:T(1,128)} %get-tuple-element.21.starts) | copy-start | bytes 1540
  18.0 22.2 %collective-permute-start.3 = (f32[128,1280]{1,0:T(8,128)}, f32[128,1280]{1,0:T(8,128)S(1)}, u32[]{:S(2)}, u32[]{:S(2)}) collective-permute-start(f32[128,1280]{1,0:T(8,128)} %get-tuple-element.33), channel_id=1, source_target_pairs={{32,0},{64,32},{96,64},{33,1},{65,33},{97,65},{34,2},{66,34},{98,6... | collective-permute-start | bytes 1966088 | tf_op jit(solution)/shard_map/ppermute | solution.py:495
  22.2 18.1 %collective-permute-start.2 = (f32[128,1280]{1,0:T(8,128)S(1)}, f32[128,1280]{1,0:T(8,128)S(1)}, u32[]{:S(2)}, u32[]{:S(2)}) collective-permute-start(f32[128,1280]{1,0:T(8,128)S(1)} %get-tuple-element.34), channel_id=1, source_target_pairs={{0,32},{32,64},{64,96},{1,33},{33,65},{65,97},{2,34},{34,66},{66,9... | collective-permute-start | bytes 1966088 | tf_op jit(solution)/shard_map/ppermute | solution.py:494

commit v2 on v1

--- a/solution.py
+++ b/solution.py
@@ -13,8 +13,7 @@
 
 
 def recip(v):
-    g = pl.reciprocal(v, approx=True)
-    return g * (2.0 - v * g)
+    return pl.reciprocal(v, approx=True)
 
 
 def angle(x, y):
@@ -71,9 +70,10 @@
         rank = rank_ref[i : i + 1, :]
         place = (rank + jnp.sum(jnp.where(mine, start, 0.0), axis=0, keepdims=True)).astype(jnp.int32)
         rank = rank.astype(jnp.int32)
-        index_ref[i : i + 1, :] = lax.shift_right_logical(place, 7)
-        index_ref[NBR + i : NBR + i + 1, :] = lax.bitwise_and(place, 127)
-        index_ref[2 * NBR + i : 2 * NBR + i + 1, :] = rank
+        index_ref[i : i + 1, :] = lax.shift_right_logical(place, 8)
+        index_ref[NBR + i : NBR + i + 1, :] = lax.bitwise_and(place, 255)
+        odd = lax.bitwise_and(owner_ref[i : i + 1, :], 1) * 128
+        index_ref[2 * NBR + i : 2 * NBR + i + 1, :] = rank + odd
         rank_hot = (sub == rank).astype(BF16)
         slot = slot_ref[i : i + 1, :] + 1
         parts = (lax.shift_right_logical(slot, 4), lax.bitwise_and(slot, 15), weight_ref[i : i + 1, :])
@@ -343,8 +343,9 @@
             Vn[j, pl.ds(p, 32, stride=8), :] = V[j, p] * (1.0 / AZ)
             rows = rows if p == 0 else rows + V[j, p]
         svf_rows.append(rows)
-    for j in range(8):
-        svf_ref[:, j * 128 : (j + 1) * 128] = Vn[j]
+    written = [pltpu.make_async_copy(Vn.at[j], svf_ref.at[:, cols(j)], sems.at[30 + j]) for j in range(8)]
+    for c in written:
+        c.start()
 
     total = jnp.zeros((224, 128), F32)
     for j in range(8):
@@ -369,49 +370,56 @@
         O[rc * 8 : rc * 8 + 8, :] = R[rc * 72 + 64 : rc * 72 + 72, :] * (weight[rc * 8 : rc * 8 + 8, :].astype(F32) * (scale / AZ))
 
     acc[...] = jnp.zeros(acc.shape, F32)
-    low = iota((128, 512), 0).astype(F32).astype(BF16)
+    low = iota((256, 512), 0).astype(F32).astype(BF16)
     zero = jnp.zeros((16, 512), BF16)
-
-    def wide(ref, row):
-        return jnp.concatenate([ref[pl.ds(row + i, 1), :] for i in range(4)], axis=1)
+    none = jnp.zeros((64, 512), BF16)
+
+    def wide(v, row, height):
+        v = jnp.concatenate([v[pl.ds(row + i, 1), :] for i in range(4)], axis=1)
+        return jnp.broadcast_to(v.astype(F32), (height, 512))
 
     def sort(g, carry):
         b = g * 4
         v = jnp.concatenate([Y[b + i] for i in range(4)], axis=1)
         v = jnp.concatenate(split2(v), axis=0)
-        o_hi, o_lo = split2(jnp.broadcast_to(wide(O, b), (128, 512)))
-        tile = jnp.broadcast_to(wide(index, b).astype(F32), (16, 512)).astype(BF16)
-        left = [jnp.where(tile == BF16(t), v, zero) for t in range(NBR)]
-        hot = (low == jnp.broadcast_to(wide(index, 32 + b).astype(F32), (128, 512)).astype(BF16)).astype(BF16)
-        acc[0:512, :] += lax.dot_general(jnp.concatenate(left, axis=0), hot, NT, preferred_element_type=F32)
-        mine = low == jnp.broadcast_to(wide(owner, b).astype(F32), (128, 512)).astype(BF16)
-        hot = (low == jnp.broadcast_to(wide(index, 64 + b).astype(F32), (128, 512)).astype(BF16)).astype(BF16)
-        left = [jnp.where(mine, o_hi, jnp.zeros_like(o_hi)), jnp.where(mine, o_lo, jnp.zeros_like(o_lo))]
-        acc[512:768, :] += lax.dot_general(jnp.concatenate(left, axis=0), hot, NT, preferred_element_type=F32)
+        tile = wide(index, b, 16).astype(BF16)
+        left = [jnp.where(tile == BF16(t), v, zero) for t in range(NBR // 2)]
+        hot = (low == wide(index, 32 + b, 256).astype(BF16)).astype(BF16)
+        acc[0:256, :] += lax.dot_general(jnp.concatenate(left, axis=0), hot, NT, preferred_element_type=F32)
+        o_hi, o_lo = split2(wide(O, b, 64))
+        mine = low[:64] == jnp.floor(wide(owner, b, 64) * 0.5).astype(BF16)
+        hot = (low == wide(index, 64 + b, 256).astype(BF16)).astype(BF16)
+        left = [jnp.where(mine, o_hi, none), jnp.where(mine, o_lo, none)]
+        acc[256:384, :] += lax.dot_general(jnp.concatenate(left, axis=0), hot, NT, preferred_element_type=F32)
         return carry
 
-    lax.fori_loop(0, NBR // 4, sort, 0, unroll=2)
+    lax.fori_loop(0, NBR // 4, sort, 0, unroll=4)
     for t in range(NBR):
-        Z[t] = acc[t * 16 : t * 16 + 8, :] + acc[t * 16 + 8 : t * 16 + 16, :]
+        r, c = t // 2 * 16, t % 2 * 128
+        Z[t] = acc[r : r + 8, c : c + 128] + acc[r + 8 : r + 16, c : c + 128]
     Z[32] = jnp.zeros((8, 128), F32)
-    out_ref[pl.ds(8, N_DEV, stride=11), :] = acc[512:640, :] + acc[640:768, :]
+    Z[33] = jnp.zeros((8, 128), F32)
+    for odd in range(2):
+        c = odd * 128
+        out_ref[pl.ds(8 + 11 * odd, 64, stride=22), :] = acc[256:320, c : c + 128] + acc[320:384, c : c + 128]
     out_ref[pl.ds(9, N_DEV, stride=11), :] = meta[0]
     out_ref[pl.ds(10, N_DEV, stride=11), :] = meta[1]
 
-    def expand(o, carry):
-        st = starts[0, o]
-        tile = lax.shift_right_logical(st, 7)
-        q = 128 - lax.bitwise_and(st, 127)
-        amount = lax.bitwise_and(q, 127)
-        after = jnp.minimum(tile + 1, 32)
-        tile = jnp.minimum(tile, 32)
-        keep = lane < q
-        a = pltpu.roll(Z[tile], amount, 1)
-        b = pltpu.roll(Z[after], amount, 1)
-        out_ref[pl.ds(o * 11, 8), :] = jnp.where(keep, a, b)
+    def expand(g, carry):
+        owners = [g * 16 + i for i in range(16)]
+        st = [starts[0, o] for o in owners]
+        tile = [lax.shift_right_logical(s, 7) for s in st]
+        q = [128 - lax.bitwise_and(s, 127) for s in st]
+        a = [pltpu.roll(Z[t], lax.bitwise_and(n, 127), 1) for t, n in zip(tile, q)]
+        b = [pltpu.roll(Z[t + 1], lax.bitwise_and(n, 127), 1) for t, n in zip(tile, q)]
+        got = [jnp.where(lane < n, u, w) for n, u, w in zip(q, a, b)]
+        for o, v in zip(owners, got):
+            out_ref[pl.ds(o * 11, 8), :] = v
         return carry
 
-    lax.fori_loop(0, N_DEV, expand, 0, unroll=8)
+    lax.fori_loop(0, N_DEV // 16, expand, 0)
+    for c in written:
+        c.wait()
 
 
 def outer(*args):
@@ -420,7 +428,7 @@
         name="outer",
         out_shape=(jax.ShapeDtypeStruct((256, 1024), F32), jax.ShapeDtypeStruct((N_DEV * 11, 128), F32)),
         in_specs=[SMEM] * 4 + [ANY] * 5 + [VMEM] * 8,
-        out_specs=[VMEM] * 2,
+        out_specs=[ANY, VMEM],
         scratch_shapes=[
             pltpu.VMEM((10, 512, 128), F32),
             pltpu.VMEM((10, 8, 64, 128), F32),
@@ -428,12 +436,12 @@
             pltpu.VMEM((8, 8, 32, 128), F32),
             pltpu.VMEM((8, 256, 128), F32),
             pltpu.VMEM((288, 128), F32),
-            pltpu.VMEM((33, 8, 128), F32),
+            pltpu.VMEM((34, 8, 128), F32),
             pltpu.VMEM((32, 8, 128), F32),
             pltpu.VMEM((32, 128), F32),
-            pltpu.VMEM((768, 128), F32),
+            pltpu.VMEM((384, 256), F32),
             pltpu.VMEM((2, 2, 4, 8, 8, 128), F32),
-            pltpu.SemaphoreType.DMA((30,)),
+            pltpu.SemaphoreType.DMA((38,)),
         ],
         compiler_params=pltpu.CompilerParams(vmem_limit_bytes=32 * 1024 * 1024),
         cost_estimate=pl.CostEstimate(flops=int(4e8), bytes_accessed=20000000, transcendentals=0),

time: 75.8 us -> 73.1 us (0.964)
  Pallas kernels: 33.8 us -> 31 us
    pallas_call x1, Pallas kernels: 14.7 us -> 12.5 us  [outer(): pl.pallas_call(outer_kernel, name='outer', out_shape=(jax.ShapeDtypeStruc...]
where the time goes in v2:
time: 73.1 us; the launch traced here: 72.8 us
  Pallas kernels  31 us (42%)
  blocking collectives  17.6 us (24%)
  starting transfers between devices  16.4 us (22%)
  waiting for transfers between devices  4.51 us (6%)
  local copies, waits for them, and re-layouts  2.21 us (3%)
  between operations  0.82 us (1%)
    all_to_all x1, blocking collectives, shards(): lax.all_to_all(packed, ('lat', 'lon'), split_axis=0, concat_axis=0, tiled...  17.6 us
    pallas_call x1, Pallas kernels, outer(): pl.pallas_call(outer_kernel, name='outer', out_shape=(jax.ShapeDtypeStruc...  12.5 us
    pallas_call x1, Pallas kernels, inner(): pl.pallas_call(inner_kernel, name='inner', out_shape=(jax.ShapeDtypeStruc...  12 us
    ppermute x1, starting transfers between devices, shards(): east = lax.ppermute(own[:, :W], 'lon', east_pairs)  7.18 us
    ppermute x1, starting transfers between devices, shards(): north = lax.ppermute(wide[rows - W:], 'lat', down)  5.11 us
    ppermute x1, waiting for transfers between devices, shards(): lax.ppermute(own[:, width - W:], 'lon', [(j, i) for i, j in east_pairs])  4.51 us
    ppermute x1, starting transfers between devices, shards(): south = lax.ppermute(wide[:W], 'lat', [(j, i) for i, j in down])  4.14 us
    pallas_call x1, Pallas kernels, route(): pl.pallas_call(route_kernel, name='route', out_shape=(jax.ShapeDtypeStruc...  3.53 us
  transfers between devices with their start and end apart: 4, of which 1 were waited for; matrix products, arithmetic and copies ran while one was open for 0% of the time, Pallas kernels for 21%

profile of v2, /device:TPU:1, one launch (start us, length us, event | category | flops | bytes accessed | tf_op | source)
XLA Modules:
  0.0 72.8 jit_solution(10971342887651542056)
XLA Ops:
  0.6 0.0 copy-start
  0.6 1.1 %fusion.1 = (f32[256,128]{1,0:T(8,128)S(1)}, f32[256,128]{1,0:T(8,128)S(1)}) fusion(f32[256,1024]{1,0:T(8,128)} %own.3), kind=kLoop, calls=%fused_computation.8 | loop fusion | bytes 524288 | tf_op jit(solution)/shard_map/slice | solution.py:495
  1.7 7.2 %collective-permute-start.1 = (f32[256,128]{1,0:T(8,128)S(1)}, f32[256,128]{1,0:T(8,128)S(1)}, u32[]{:S(2)}, u32[]{:S(2)}) collective-permute-start(f32[256,128]{1,0:T(8,128)S(1)} %get-tuple-element.35), channel_id=1, source_target_pairs={{1,0},{2,1},{3,2},{4,3},{5,4},{6,5},{7,6},{8,7},{9,8},{10,9},{11,1... | collective-permute-start | bytes 393224 | tf_op jit(solution)/shard_map/ppermute | solution.py:495
  8.9 0.0 collective-permute-start
  8.9 3.5 %route.1 = (s32[1,128]{1,0:T(1,128)}, s32[96,128]{1,0:T(8,128)}, f32[2,128,128]{2,1,0:T(8,128)}) custom-call(s32[32,128]{1,0:T(8,128)} %bitcast.9, s32[32,128]{1,0:T(8,128)} %bitcast.13, s32[32,128]{1,0:T(8,128)} %bitcast.11), custom_call_target="tpu_custom_call" | custom-call | flops 400000000 | bytes 200000 | tf_op jit(solution)/shard_map/route/pallas_call | solution.py:87
  12.4 0.0 collective-permute-done.1.east
  12.4 4.5 %collective-permute-done.west = f32[256,128]{1,0:T(8,128)S(1)} collective-permute-done((f32[256,128]{1,0:T(8,128)S(1)}, f32[256,128]{1,0:T(8,128)S(1)}, u32[]{:S(2)}, u32[]{:S(2)}) %collective-permute-start) | collective-permute-done | bytes 131104 | tf_op jit(solution)/shard_map/ppermute | solution.py:494
  17.0 0.0 copy-done
  17.0 0.1 constant_dynamic-update-slice_fusion.1
  17.1 0.0 copy-start.5
  17.1 0.9 %fusion = (f32[128,1280]{1,0:T(8,128)}, f32[128,1280]{1,0:T(8,128)S(1)}) fusion(f32[256,1280]{1,0:T(8,128)S(1)} %constant_dynamic-update-slice_fusion), kind=kLoop, calls=%fused_computation.7 | loop fusion | bytes 2621440 | tf_op jit(solution)/shard_map/slice | solution.py:503
  18.0 0.0 copy-start.1
  18.0 0.0 copy-start.2
  18.0 0.0 copy-start.3
  18.0 0.0 copy-start.4
  18.0 0.0 copy-start.6
  18.0 4.1 %collective-permute-start.3 = (f32[128,1280]{1,0:T(8,128)}, f32[128,1280]{1,0:T(8,128)S(1)}, u32[]{:S(2)}, u32[]{:S(2)}) collective-permute-start(f32[128,1280]{1,0:T(8,128)} %get-tuple-element.33), channel_id=1, source_target_pairs={{32,0},{64,32},{96,64},{33,1},{65,33},{97,65},{34,2},{66,34},{98,6... | collective-permute-start | bytes 1966088 | tf_op jit(solution)/shard_map/ppermute | solution.py:503
  22.2 5.1 %collective-permute-start.2 = (f32[128,1280]{1,0:T(8,128)S(1)}, f32[128,1280]{1,0:T(8,128)S(1)}, u32[]{:S(2)}, u32[]{:S(2)}) collective-permute-start(f32[128,1280]{1,0:T(8,128)S(1)} %get-tuple-element.34), channel_id=1, source_target_pairs={{0,32},{32,64},{64,96},{1,33},{33,65},{65,97},{2,34},{34,66},{66,9... | collective-permute-start | bytes 1966088 | tf_op jit(solution)/shard_map/ppermute | solution.py:502
  27.3 0.1 pad_add_fusion.lat
  27.4 0.1 multiply_rsqrt_fusion.inv_row
  27.4 0.1 add_rsqrt_fusion
  27.5 0.0 copy-done.5
  27.5 0.1 broadcast_in_dim.2.inv_base
  27.6 12.0 %inner.1 = (f32[8,8,32,128]{3,2,1,0:T(8,128)S(1)}, f32[4,3,8,8,128]{4,3,2,1,0:T(8,128)S(1)}, f32[2,32,128]{2,1,0:T(8,128)S(1)}) custom-call(s32[8,8]{1,0:T(8,128)S(1)} %copy-done.5, f32[8,8]{1,0:T(8,128)S(1)} %convert_divide_fusion.inv_lags, f32[256,1024]{1,0:T(8,128)S(1)} %copy-done, f32[256,128]{1,0:T(8,128)S(1)} %collective-permute-done.west, ...), custom_call_target="tpu_custom_call" | custom-call | flops 400000000 | bytes 30000000 | tf_op jit(solution)/shard_map/inner/pallas_call | solution.py:277
  39.6 0.0 collective-permute-done.3.south
  39.6 0.0 collective-permute-done.2.north
  39.7 0.0 copy-done.1
  39.7 0.0 copy-done.2
  39.7 0.0 copy-done.3
  39.7 0.0 copy-done.4
  39.7 0.0 copy-done.6
  39.7 12.5 %outer.1 = (f32[256,1024]{1,0:T(8,128)}, f32[1408,128]{1,0:T(8,128)S(1)}) custom-call(s32[8,8]{1,0:T(8,128)S(1)} %copy-done.5, f32[8,8]{1,0:T(8,128)S(1)} %convert_divide_fusion.inv_lags, s32[1,128]{1,0:T(1,128)S(1)} %copy-done.6, s32[2]{0:T(128)S(1)} %pad_add_fusion.lat, f32[256,1024]{1,0:T(8,128)S(1)} %copy-done, ...), custom_call_target="tpu_custom_call" | custom-call | flops 400000000 | bytes 20000000 | tf_op jit(solution)/shard_map/outer/pallas_call | solution.py:426
  52.2 17.6 %all_to_all.5 = f32[128,1,1408]{2,1,0:T(1,128)S(1)} all-to-all(f32[128,1,1408]{2,1,0:T(1,128)S(1)} %bitcast.8), channel_id=1, replica_groups=mesh['lat'=4,'lon'=32] {'lat','lon'}, dimensions={0} | all-to-all | bytes 1441792 | tf_op jit(solution)/shard_map/all_to_all | solution.py:520
  69.8 3.0 %cells.1 = (f32[8,512]{1,0:T(8,128)}, f32[1,512]{1,0:T(1,128)}) custom-call(f32[1408,128]{1,0:T(8,128)S(1)} %bitcast.7), custom_call_target="tpu_custom_call" | custom-call | tf_op jit(solution)/shard_map/cells/pallas_call | solution.py:477
  (3 shorter events, 0.0 us)
Async XLA Ops:
  0.6 16.3 %copy-start = (f32[256,1024]{1,0:T(8,128)S(1)}, f32[256,1024]{1,0:T(8,128)}, u32[]{:S(2)}) copy-start(f32[256,1024]{1,0:T(8,128)} %own.3) | copy-start | bytes 3145732
  1.7 10.7 %collective-permute-start.1 = (f32[256,128]{1,0:T(8,128)S(1)}, f32[256,128]{1,0:T(8,128)S(1)}, u32[]{:S(2)}, u32[]{:S(2)}) collective-permute-start(f32[256,128]{1,0:T(8,128)S(1)} %get-tuple-element.35), channel_id=1, source_target_pairs={{1,0},{2,1},{3,2},{4,3},{5,4},{6,5},{7,6},{8,7},{9,8},{10,9},{11,1... | collective-permute-start | bytes 393224 | tf_op jit(solution)/shard_map/ppermute | solution.py:495
  8.9 8.0 %collective-permute-start = (f32[256,128]{1,0:T(8,128)S(1)}, f32[256,128]{1,0:T(8,128)S(1)}, u32[]{:S(2)}, u32[]{:S(2)}) collective-permute-start(f32[256,128]{1,0:T(8,128)S(1)} %get-tuple-element.36), channel_id=1, source_target_pairs={{0,1},{1,2},{2,3},{3,4},{4,5},{5,6},{6,7},{7,8},{8,9},{9,10},{10,1... | collective-permute-start | bytes 393224 | tf_op jit(solution)/shard_map/ppermute | solution.py:494
  17.1 10.4 %copy-start.5 = (s32[8,8]{1,0:T(8,128)S(1)}, s32[8,8]{1,0:T(8,128)}, u32[]{:S(2)}) copy-start(s32[8,8]{1,0:T(8,128)} %lags.3) | copy-start | bytes 772
  18.0 21.7 %copy-start.1 = (f32[2,128,128]{2,1,0:T(8,128)S(1)}, f32[2,128,128]{2,1,0:T(8,128)}, u32[]{:S(2)}) copy-start(f32[2,128,128]{2,1,0:T(8,128)} %get-tuple-element.28.meta) | copy-start | bytes 393220
  18.0 21.7 %copy-start.2 = (s32[96,128]{1,0:T(8,128)S(1)}, s32[96,128]{1,0:T(8,128)}, u32[]{:S(2)}) copy-start(s32[96,128]{1,0:T(8,128)} %get-tuple-element.27.index) | copy-start | bytes 147460
  18.0 21.7 %copy-start.3 = (s32[4096,1]{0,1:T(1,128)S(1)}, s32[4096,1]{0,1:T(1,128)}, u32[]{:S(2)}) copy-start(s32[4096,1]{0,1:T(1,128)} %param.7) | copy-start | bytes 49156
  18.0 21.7 %copy-start.4 = (s32[4096]{0:T(1024)S(1)}, s32[4096]{0:T(1024)}, u32[]{:S(2)}) copy-start(s32[4096]{0:T(1024)} %param.9) | copy-start | bytes 49156
  18.0 21.7 %copy-start.6 = (s32[1,128]{1,0:T(1,128)S(1)}, s32[1,128]{1,0:T(1,128)}, u32[]{:S(2)}) copy-start(s32[1,128]{1,0:T(1,128)} %get-tuple-element.21.starts) | copy-start | bytes 1540
  18.0 21.6 %collective-permute-start.3 = (f32[128,1280]{1,0:T(8,128)}, f32[128,1280]{1,0:T(8,128)S(1)}, u32[]{:S(2)}, u32[]{:S(2)}) collective-permute-start(f32[128,1280]{1,0:T(8,128)} %get-tuple-element.33), channel_id=1, source_target_pairs={{32,0},{64,32},{96,64},{33,1},{65,33},{97,65},{34,2},{66,34},{98,6... | collective-permute-start | bytes 1966088 | tf_op jit(solution)/shard_map/ppermute | solution.py:503
  22.2 17.5 %collective-permute-start.2 = (f32[128,1280]{1,0:T(8,128)S(1)}, f32[128,1280]{1,0:T(8,128)S(1)}, u32[]{:S(2)}, u32[]{:S(2)}) collective-permute-start(f32[128,1280]{1,0:T(8,128)S(1)} %get-tuple-element.34), channel_id=1, source_target_pairs={{0,32},{32,64},{64,96},{1,33},{33,65},{65,97},{2,34},{34,66},{66,9... | collective-permute-start | bytes 1966088 | tf_op jit(solution)/shard_map/ppermute | solution.py:502

commit v3 on v2

--- a/solution.py
+++ b/solution.py
@@ -106,16 +106,16 @@
 
 
 class Ray:
-    def __init__(self, azimuth, step, near, far, inv_base, opening, put):
-        self.azimuth, self.step, self.near, self.far = azimuth, step, near, far
+    def __init__(self, azimuth, near, far, inv_base, opening, put):
+        self.azimuth, self.near, self.far = azimuth, near, far
         self.inv_base, self.opening, self.put = inv_base, opening, put
 
 
-def plane_rays(H, it, h0, rays, inv_base, V_old, V, S_ref):
+def plane_rays(tile, it, h0, rays, inv_base, V_old, V, S_ref):
     lane = iota((8, 128), 1)
     rc = lax.shift_right_logical(it, 1)
     p0 = lax.bitwise_and(it, 1) * 4
-    block = pl.multiple_of(rc * 8, 8)
+    block = pl.ds(pl.multiple_of(rc * 8, 8), 8)
     made = []
     for f, (a, sy, sx) in enumerate(rays):
         off = 1 if sx >= 0 else 0
@@ -123,12 +123,12 @@
 
         def near(p):
             rows = pl.ds(pl.multiple_of(h0 // 8 + rc * 8, 8), 8)
-            return [H[1 + j, p0 + p, rows, :] for j in range(8)]
+            return [tile(1 + j, p0 + p, rows) for j in range(8)]
 
         def far(p, s, sy=sy, sx=sx, off=off, count=count):
             y = h0 + rc * 64 + p0 + p + sy * s
             plane, i0 = lax.bitwise_and(y, 7), lax.shift_right_logical(y, 3)
-            tiles = [H[off + j, plane, pl.ds(i0, 8), :] for j in range(count)]
+            tiles = [tile(off + j, plane, pl.ds(i0, 8)) for j in range(count)]
             if sx == 0:
                 return tiles
             amount = 128 - s if sx == 1 else lax.bitwise_and(s, 127)
@@ -137,50 +137,49 @@
             return [jnp.where(keep, rolled[j], rolled[j + 1]) for j in range(8)]
 
         def base(p, sx=sx):
-            return 1.0 / pixel_size if sx == 0 else inv_base[p0 + p, pl.ds(block, 8), :]
+            return 1.0 / pixel_size if sx == 0 else inv_base[p0 + p, block, :]
 
         def opening(p, j, v, f=f):
             old = V_old if f == 0 else V
-            at = (j, p0 + p, pl.ds(block, 8))
+            at = (j, p0 + p, block)
             V[at] = v if old is None else old[at] + v
 
         def put(j, v, f=f):
             S_ref[rc, f, j] += v
 
-        made.append(Ray(a, sy, near, far, base, opening, put))
+        made.append(Ray(a, near, far, base, opening, put))
     return made
 
 
-def turned_rays(H, it, inv_row, V, S_ref):
+def turned_ray(T, first, it, facing, inv_row, V_old, V, S_ref):
     rt = lax.shift_right_logical(it, 2)
     half = lax.bitwise_and(lax.shift_right_logical(it, 1), 1)
     p0 = lax.bitwise_and(it, 1) * 4
-    made = []
-    for f, (a, sx) in enumerate(((0, 1), (4, -1))):
-
-        def near(p):
-            return [H[rt, p0 + p, pl.ds(pl.multiple_of(16 + half * 64 + 8 * j, 8), 8), :] for j in range(8)]
-
-        def far(p, s, sx=sx):
-            x = 128 + half * 512 + p0 + p + sx * s
-            plane, i0 = lax.bitwise_and(x, 7), lax.shift_right_logical(x, 3)
-            return [H[rt, plane, pl.ds(i0 + 8 * j, 8), :] for j in range(8)]
-
-        def base(p):
-            return jnp.broadcast_to(inv_row[pl.ds(rt, 1), :], (8, 128))
-
-        def rows(j):
-            return pl.ds(pl.multiple_of(half * 64 + 8 * j, 8), 8)
-
-        def opening(p, j, v, f=f):
-            at = (rt, p0 + p, rows(j))
-            V[at] = v if f == 0 else V[at] + v
-
-        def put(j, v, f=f):
-            S_ref[rt, f, rows(j), :] += v
-
-        made.append(Ray(a, sx, near, far, base, opening, put))
-    return made
+    west = lax.bitwise_xor(half, facing)
+    sx = 1 - 2 * west
+
+    def rows(j):
+        return pl.ds(pl.multiple_of(half * 64 + 8 * j, 8), 8)
+
+    def near(p):
+        return [T[rt, p0 + p, pl.ds(pl.multiple_of(first + half * 64 + 8 * j, 8), 8), :] for j in range(8)]
+
+    def far(p, s):
+        x = 8 * first + half * 512 + p0 + p + sx * s
+        plane, i0 = lax.bitwise_and(x, 7), lax.shift_right_logical(x, 3)
+        return [T[rt, plane, pl.ds(i0 + 8 * j, 8), :] for j in range(8)]
+
+    def base(p):
+        return jnp.broadcast_to(inv_row[pl.ds(rt, 1), :], (8, 128))
+
+    def opening(p, j, v):
+        at = (rt, p0 + p, rows(j))
+        V[at] = v if V_old is None else V_old[at] + v
+
+    def put(j, v):
+        S_ref[rt, rows(j), :] += v
+
+    return Ray(4 * west, near, far, base, opening, put)
 
 
 def march(lags, inv_lags, group, rise):
@@ -226,39 +225,91 @@
     return pl.ds(j * 128, 128)
 
 
-def inner_kernel(
-    lags, inv_lags, own, west, east, inv_base, inv_row, V_ref, S_ref, pooled_ref, Hn, H, Tn, T, VT, ST, X, Xn, rise, sems
-):
-    copies(
-        [(own.at[:, cols(j)], Hn.at[1 + j]) for j in range(8)] + [(west, Hn.at[0]), (east, Hn.at[9])], sems
-    )
-    for c in range(10):
+def first_kernel(lags, inv_lags, own, inv_row, H, T, V, S_ref, VT, ST, Hn, Tn, rise, sems):
+    copies([(own.at[:, cols(j)], Hn.at[j]) for j in range(8)], sems)
+    for c in range(8):
         for p in range(8):
             H[c, p] = Hn[c, pl.ds(p, 32, stride=8), :]
         for rt in range(2):
             Tn[rt, c * 128 : (c + 1) * 128, :] = Hn[c, rt * 128 : (rt + 1) * 128, :].T
     for rt in range(2):
         for p in range(8):
-            T[rt, p] = Tn[rt, pl.ds(p, 160, stride=8), :]
+            T[rt, p] = Tn[rt, pl.ds(p, 128, stride=8), :]
     S_ref[...] = jnp.zeros(S_ref.shape, F32)
     ST[...] = jnp.zeros(ST.shape, F32)
 
+    def tile(c, p, rows):
+        return H[c - 1, p, rows, :]
+
     def step(it, carry):
-        left, up, right = plane_rays(H, it, 0, slanted(it < 4), inv_base, None, V_ref, S_ref)
-        along, against = turned_rays(T, it, inv_row, VT, ST)
-        groups = ((left, along), (right, against), (up,))
-        order = (0, 2, 1)
+        up = plane_rays(tile, it, 0, slanted(it < 4)[1:2], None, None, V, S_ref)
+        group = up + [turned_ray(T, 0, it, 0, inv_row, None, VT, ST)]
+        march(lags, inv_lags, group, rise)
+        finish(group, rise)
+        return carry
+
+    lax.fori_loop(0, 8, step, 0)
+
+
+def first(*args):
+    return pl.pallas_call(
+        first_kernel,
+        name="first",
+        out_shape=(
+            jax.ShapeDtypeStruct((8, 8, 32, 128), F32),
+            jax.ShapeDtypeStruct((2, 8, 128, 128), F32),
+            jax.ShapeDtypeStruct((8, 8, 32, 128), F32),
+            jax.ShapeDtypeStruct((4, 1, 8, 8, 128), F32),
+            jax.ShapeDtypeStruct((2, 8, 128, 128), F32),
+            jax.ShapeDtypeStruct((2, 128, 128), F32),
+        ),
+        in_specs=[SMEM] * 2 + [ANY, VMEM],
+        out_specs=[VMEM] * 6,
+        scratch_shapes=[
+            pltpu.VMEM((8, 256, 128), F32),
+            pltpu.VMEM((2, 1024, 128), F32),
+            pltpu.VMEM((2, 4, 8, 8, 128), F32),
+            pltpu.SemaphoreType.DMA((8,)),
+        ],
+        compiler_params=pltpu.CompilerParams(vmem_limit_bytes=24 * 1024 * 1024),
+        cost_estimate=pl.CostEstimate(flops=int(1e8), bytes_accessed=10000000, transcendentals=0),
+    )(*args)
+
+
+def inner_kernel(
+    lags, inv_lags, west, east, inv_base, inv_row, H, T_own, V_old, VT_old, ST_old,
+    V_ref, S_ref, pooled_ref, E, Tn, T, VT, ST, X, Xn, rise, sems,
+):
+    own = pltpu.make_async_copy(T_own, T.at[:, :, pl.ds(16, 128)], sems.at[0])
+    own.start()
+    for side, edge in enumerate((west, east)):
+        for p in range(8):
+            E[side, p] = edge[pl.ds(p, 32, stride=8), :]
+        for rt in range(2):
+            Tn[side, rt] = edge[rt * 128 : (rt + 1) * 128, :].T
+            for p in range(8):
+                T[rt, p, 144 * side : 144 * side + 16, :] = Tn[side, rt, pl.ds(p, 16, stride=8), :]
+    S_ref[...] = jnp.zeros(S_ref.shape, F32)
+    ST[...] = jnp.zeros(ST.shape, F32)
+    own.wait()
+
+    def tile(c, p, rows):
+        return H[c - 1, p, rows, :] if 1 <= c <= 8 else E[c // 9, p, rows, :]
+
+    def step(it, carry):
+        left, right = plane_rays(tile, it, 0, slanted(it < 4)[::2], inv_base, V_old, V_ref, S_ref)
+        groups = ((left, turned_ray(T, 16, it, 1, inv_row, VT_old, VT, ST)), (right,))
         for n, g in enumerate(groups):
             march(lags, inv_lags, g, rise.at[n])
-        for n in order:
-            finish(groups[n], rise.at[n])
+        for n, g in enumerate(groups):
+            finish(g, rise.at[n])
         return carry
 
     lax.fori_loop(0, 8, step, 0)
     pool = (iota((16, 128), 0) == lax.shift_right_logical(iota((16, 128), 1), 3)).astype(BF16)
     for rt in range(2):
-        for f in range(2):
-            hi, lo = split2(ST[rt, f])
+        for f, (lower, upper) in enumerate(((ST_old, ST), (ST, ST_old))):
+            hi, lo = split2(jnp.concatenate([lower[rt, 0:64, :], upper[rt, 64:128, :]], axis=0))
             total = lax.dot_general(pool, hi, NT, preferred_element_type=F32)
             pooled_ref[f, rt * 16 : rt * 16 + 16, :] = total + lax.dot_general(pool, lo, NT, preferred_element_type=F32)
         for c in range(8):
@@ -279,22 +330,21 @@
         name="inner",
         out_shape=(
             jax.ShapeDtypeStruct((8, 8, 32, 128), F32),
-            jax.ShapeDtypeStruct((4, 3, 8, 8, 128), F32),
+            jax.ShapeDtypeStruct((4, 2, 8, 8, 128), F32),
             jax.ShapeDtypeStruct((2, NBR, 128), F32),
         ),
-        in_specs=[SMEM] * 2 + [ANY] * 3 + [VMEM] * 2,
+        in_specs=[SMEM] * 2 + [VMEM] * 9,
         out_specs=[VMEM] * 3,
         scratch_shapes=[
-            pltpu.VMEM((10, 256, 128), F32),
-            pltpu.VMEM((10, 8, 32, 128), F32),
-            pltpu.VMEM((2, 1280, 128), F32),
+            pltpu.VMEM((2, 8, 32, 128), F32),
+            pltpu.VMEM((2, 2, 128, 128), F32),
             pltpu.VMEM((2, 8, 160, 128), F32),
             pltpu.VMEM((2, 8, 128, 128), F32),
-            pltpu.VMEM((2, 2, 128, 128), F32),
+            pltpu.VMEM((2, 128, 128), F32),
             pltpu.VMEM((2, 8, 128, 128), F32),
             pltpu.VMEM((2, 8, 128, 128), F32),
-            pltpu.VMEM((3, 2, 4, 8, 8, 128), F32),
-            pltpu.SemaphoreType.DMA((10,)),
+            pltpu.VMEM((2, 2, 4, 8, 8, 128), F32),
+            pltpu.SemaphoreType.DMA((1,)),
         ],
         compiler_params=pltpu.CompilerParams(vmem_limit_bytes=32 * 1024 * 1024),
         cost_estimate=pl.CostEstimate(flops=int(4e8), bytes_accessed=30000000, transcendentals=0),
@@ -302,7 +352,7 @@
 
 
 def outer_kernel(
-    lags, inv_lags, starts, lat, own, north, south, west, east, inv_base, V_in, S_in, pooled, weight, owner, index, meta,
+    lags, inv_lags, starts, lat, own, north, south, west, east, inv_base, V_in, S_in, S_up, pooled, weight, owner, index, meta,
     svf_ref, out_ref, Hn, H, S, V, Vn, R, Z, Y, O, acc, rise, sems,
 ):
     pairs = [(own.at[:, cols(j)], Hn.at[1 + j, pl.ds(128, 256)]) for j in range(8)]
@@ -326,8 +376,11 @@
             H[c, p] = Hn[c, pl.ds(p, 64, stride=8), :]
     S[...] = jnp.zeros(S.shape, F32)
 
+    def tile(c, p, rows):
+        return H[c, p, rows, :]
+
     def step(it, carry):
-        left, up, right = plane_rays(H, it, 128, slanted(it >= 4), inv_base, V_in, V, S)
+        left, up, right = plane_rays(tile, it, 128, slanted(it >= 4), inv_base, V_in, V, S)
         groups = ((left, up), (right,))
         for n, g in enumerate(groups):
             march(lags, inv_lags, g, rise.at[n])
@@ -352,8 +405,9 @@
         pool = (iota((128, 128), 1) == j * 16 + lax.shift_right_logical(iota((128, 128), 0), 3)).astype(BF16)
         field = []
         for rc in range(4):
-            south, north_ = (S_in, S) if rc < 2 else (S, S_in)
-            field += [south[rc, 2, j], south[rc, 1, j], south[rc, 0, j], north_[rc, 0, j], north_[rc, 1, j], north_[rc, 2, j]]
+            near = [S_in[rc, 0, j], S_up[rc, 0, j], S_in[rc, 1, j]]
+            away = [S[rc, f, j] for f in range(3)]
+            field += near[::-1] + away if rc < 2 else away[::-1] + near
             field.append(svf_rows[j][rc * 8 : rc * 8 + 8, :])
         hi, lo = split2(jnp.concatenate(field, axis=0))
         total = total + jnp.dot(hi, pool, preferred_element_type=F32) + jnp.dot(lo, pool, preferred_element_type=F32)
@@ -427,7 +481,7 @@
         outer_kernel,
         name="outer",
         out_shape=(jax.ShapeDtypeStruct((256, 1024), F32), jax.ShapeDtypeStruct((N_DEV * 11, 128), F32)),
-        in_specs=[SMEM] * 4 + [ANY] * 5 + [VMEM] * 8,
+        in_specs=[SMEM] * 4 + [ANY] * 5 + [VMEM] * 9,
         out_specs=[ANY, VMEM],
         scratch_shapes=[
             pltpu.VMEM((10, 512, 128), F32),
@@ -496,24 +550,27 @@
     weight = footprint_weight.reshape(NBR, 128)
     owner = holder_devices.reshape(NBR, 128)
     start, index, meta = route(owner, holder_region_slot.reshape(NBR, 128), weight)
-    west, east, start, index, meta = lax.optimization_barrier((west, east, start, index, meta))
-    wide = jnp.concatenate([west, own, east], axis=1)
-    down = [(i, i + 1) for i in range(n_lat - 1)]
-    north = lax.ppermute(wide[rows - W :], "lat", down)
-    south = lax.ppermute(wide[:W], "lat", [(j, i) for i, j in down])
-
     rows_global = (lax.axis_index("lat") * rows + jnp.arange(rows, dtype=jnp.int32)).astype(F32)
     latitude = 47.0 - (rows_global + 0.5) / 1200.0
     coslat = jnp.cos(latitude * jnp.pi / 180.0)
     across = (pixel_size * coslat) ** 2
     inv_row = (1.0 / jnp.sqrt(across)).reshape(2, 128)
+    inv_lags = 1.0 / azimuth_lag_tallies.astype(F32)
+    straight, turned, part, up, turned_part, turned_sums = first(azimuth_lag_tallies, inv_lags, own, inv_row)
+    west, east, start, index, meta, part = lax.optimization_barrier((west, east, start, index, meta, part))
+    wide = jnp.concatenate([west, own, east], axis=1)
+    down = [(i, i + 1) for i in range(n_lat - 1)]
+    north = lax.ppermute(wide[rows - W :], "lat", down)
+    south = lax.ppermute(wide[:W], "lat", [(j, i) for i, j in down])
+
     inv_base = 1.0 / jnp.sqrt(pixel_size**2 + across)
     inv_base = jnp.broadcast_to(inv_base.reshape(32, 8).T[:, :, None], (8, 32, 128))
     lat = jnp.stack([lax.axis_index("lat").astype(jnp.int32), jnp.int32(n_lat)])
-    inv_lags = 1.0 / azimuth_lag_tallies.astype(F32)
-    part, sums, pooled = inner(azimuth_lag_tallies, inv_lags, own, west, east, inv_base, inv_row)
+    part, sums, pooled = inner(
+        azimuth_lag_tallies, inv_lags, west, east, inv_base, inv_row, straight, turned, part, turned_part, turned_sums
+    )
     fine_svf, packed = outer(
-        azimuth_lag_tallies, inv_lags, start, lat, own, north, south, west, east, inv_base, part, sums, pooled,
+        azimuth_lag_tallies, inv_lags, start, lat, own, north, south, west, east, inv_base, part, sums, up, pooled,
         weight, owner, index, meta,
     )
     packed = packed.reshape(N_DEV, 1, 11 * 128)

time: 73.1 us -> 81.1 us (1.11)
  blocking collectives: 17.6 us -> 24.4 us
  waiting for transfers between devices: 4.51 us -> 0.01 us
  local copies, waits for them, and re-layouts: 2.21 us -> 6.55 us
  Pallas kernels: 31 us -> 32.8 us
  starting transfers between devices: 16.4 us -> 15.2 us
    all_to_all x1, blocking collectives: 17.6 us -> 24.4 us  [shards(): lax.all_to_all(packed, ('lat', 'lon'), split_axis=0, concat_axis=0, tiled...]
    pallas_call x0 -> x1, Pallas kernels: none -> 5.29 us  [first(): pl.pallas_call(first_kernel, name='first', out_shape=(jax.ShapeDtypeStruc...]
    unnamed x16 -> x32, local copies, waits for them, and re-layouts: 0.12 us -> 4.66 us
    ppermute x1, waiting for transfers between devices: 4.51 us -> 0.01 us  [shards(): lax.ppermute(own[:, width - W:], 'lon', [(j, i) for i, j in east_pairs])]
    pallas_call x1, Pallas kernels: 12 us -> 8.52 us  [inner(): pl.pallas_call(inner_kernel, name='inner', out_shape=(jax.ShapeDtypeStruc...]
    ppermute x1, starting transfers between devices: 4.14 us -> 3.01 us  [shards(): south = lax.ppermute(wide[:W], 'lat', [(j, i) for i, j in down])]
    slice x1, local copies, waits for them, and re-layouts: 0.92 us -> 0.09 us  [shards(): south = lax.ppermute(wide[:W], 'lat', [(j, i) for i, j in down])]
  transfers between devices with their start and end apart: 4 -> 4, of which waited for: 1 -> 0; matrix products, arithmetic and copies ran while one was open for 0% -> 1% of each run, Pallas kernels for 21% -> 21%
where the time goes in v3:
time: 81.1 us; the launch traced here: 80.8 us
  Pallas kernels  32.8 us (40%)
  blocking collectives  24.4 us (30%)
  starting transfers between devices  15.2 us (19%)
  local copies, waits for them, and re-layouts  6.55 us (8%)
  between operations  0.9 us (1%)
  other arithmetic  0.88 us (1%)
    all_to_all x1, blocking collectives, shards(): lax.all_to_all(packed, ('lat', 'lon'), split_axis=0, concat_axis=0, tiled...  24.4 us
    pallas_call x1, Pallas kernels, outer(): pl.pallas_call(outer_kernel, name='outer', out_shape=(jax.ShapeDtypeStruc...  12.5 us
    pallas_call x1, Pallas kernels, inner(): pl.pallas_call(inner_kernel, name='inner', out_shape=(jax.ShapeDtypeStruc...  8.52 us
    ppermute x1, starting transfers between devices, shards(): east = lax.ppermute(own[:, :W], 'lon', east_pairs)  7.11 us
    pallas_call x1, Pallas kernels, first(): pl.pallas_call(first_kernel, name='first', out_shape=(jax.ShapeDtypeStruc...  5.29 us
    ppermute x1, starting transfers between devices, shards(): north = lax.ppermute(wide[rows - W:], 'lat', down)  5.1 us
    unnamed x32, local copies, waits for them, and re-layouts  4.66 us
    pallas_call x1, Pallas kernels, route(): pl.pallas_call(route_kernel, name='route', out_shape=(jax.ShapeDtypeStruc...  3.51 us
  transfers between devices with their start and end apart: 4, of which 0 were waited for; matrix products, arithmetic and copies ran while one was open for 1% of the time, Pallas kernels for 21%

profile of v3, /device:TPU:1, one launch (start us, length us, event | category | flops | bytes accessed | tf_op | source)
XLA Modules:
  0.0 80.8 jit_solution(9056141402919453632)
XLA Ops:
  0.6 1.7 %fusion.1 = (f32[256,128]{1,0:T(8,128)}, f32[256,128]{1,0:T(8,128)}) fusion(f32[256,1024]{1,0:T(8,128)} %own.3), kind=kLoop, calls=%fused_computation.8 | loop fusion | bytes 524288 | tf_op jit(solution)/shard_map/slice | solution.py:549
  2.3 7.1 %collective-permute-start.1 = (f32[256,128]{1,0:T(8,128)}, f32[256,128]{1,0:T(8,128)S(1)}, u32[]{:S(2)}, u32[]{:S(2)}) collective-permute-start(f32[256,128]{1,0:T(8,128)} %get-tuple-element.49), channel_id=1, source_target_pairs={{1,0},{2,1},{3,2},{4,3},{5,4},{6,5},{7,6},{8,7},{9,8},{10,9},{11,1... | collective-permute-start | bytes 393224 | tf_op jit(solution)/shard_map/ppermute | solution.py:549
  9.4 0.0 collective-permute-start
  9.4 0.7 convert_divide_fusion.inv_lags
  10.1 0.1 multiply_rsqrt_fusion.inv_row
  10.2 0.0 copy-start
  10.2 1.2 %copy-done = f32[256,1024]{1,0:T(8,128)S(1)} copy-done((f32[256,1024]{1,0:T(8,128)S(1)}, f32[256,1024]{1,0:T(8,128)}, u32[]{:S(2)}) %copy-start) | copy-done | bytes 1048600
  11.4 0.7 copy-done.9
  12.1 5.3 %first.1 = (f32[8,8,32,128]{3,2,1,0:T(8,128)S(1)}, f32[2,8,128,128]{3,2,1,0:T(8,128)S(1)}, f32[8,8,32,128]{3,2,1,0:T(8,128)S(1)}, f32[4,1,8,8,128]{4,3,2,1,0:T(8...) custom-call(s32[8,8]{1,0:T(8,128)S(1)} %copy-done.9, f32[8,8]{1,0:T(8,128)S(1)} %convert_divide_fusion.inv_lags, ...), custom_call_target="tpu_custom_call" | custom-call | flops 100000000 | bytes 10000000 | tf_op jit(solution)/shard_map/first/pallas_call | solution.py:255
  17.4 0.0 copy-start.2
  17.4 1.0 %copy-done.2 = f32[8,8,32,128]{3,2,1,0:T(8,128)} copy-done((f32[8,8,32,128]{3,2,1,0:T(8,128)}, f32[8,8,32,128]{3,2,1,0:T(8,128)S(1)}, u32[]{:S(2)}) %copy-start.2) | copy-done | bytes 1048600
  18.4 1.0 %copy-done.4 = f32[2,8,128,128]{3,2,1,0:T(8,128)} copy-done((f32[2,8,128,128]{3,2,1,0:T(8,128)}, f32[2,8,128,128]{3,2,1,0:T(8,128)S(1)}, u32[]{:S(2)}) %copy-start.4) | copy-done | bytes 1048600
  19.4 0.6 copy-done.7
  20.0 3.5 %route.1 = (s32[1,128]{1,0:T(1,128)}, s32[96,128]{1,0:T(8,128)}, f32[2,128,128]{2,1,0:T(8,128)}) custom-call(s32[32,128]{1,0:T(8,128)} %bitcast.9, s32[32,128]{1,0:T(8,128)} %bitcast.13, s32[32,128]{1,0:T(8,128)} %bitcast.11), custom_call_target="tpu_custom_call" | custom-call | flops 400000000 | bytes 200000 | tf_op jit(solution)/shard_map/route/pallas_call | solution.py:87
  23.5 0.0 collective-permute-done.1.east
  23.5 0.0 collective-permute-done.west
  23.6 0.0 copy-done.1
  23.6 0.1 constant_dynamic-update-slice_fusion.1
  23.7 0.0 copy-start.3
  23.7 0.0 copy-start.5
  23.7 0.0 copy-start.8
  23.7 0.0 copy-start.10
  23.7 0.1 fusion
  23.8 3.0 %collective-permute-start.3 = (f32[128,1280]{1,0:T(8,128)S(1)}, f32[128,1280]{1,0:T(8,128)S(1)}, u32[]{:S(2)}, u32[]{:S(2)}) collective-permute-start(f32[128,1280]{1,0:T(8,128)S(1)} %get-tuple-element.47), channel_id=1, source_target_pairs={{32,0},{64,32},{96,64},{33,1},{65,33},{97,65},{34,2},{66,34},{98,6... | collective-permute-start | bytes 1966088 | tf_op jit(solution)/shard_map/ppermute | solution.py:564
  26.8 5.1 %collective-permute-start.2 = (f32[128,1280]{1,0:T(8,128)S(1)}, f32[128,1280]{1,0:T(8,128)S(1)}, u32[]{:S(2)}, u32[]{:S(2)}) collective-permute-start(f32[128,1280]{1,0:T(8,128)S(1)} %get-tuple-element.48), channel_id=1, source_target_pairs={{0,32},{32,64},{64,96},{1,33},{33,65},{65,97},{2,34},{34,66},{66,9... | collective-permute-start | bytes 1966088 | tf_op jit(solution)/shard_map/ppermute | solution.py:563
  31.9 0.1 pad_add_fusion.lat
  32.0 0.1 add_rsqrt_fusion
  32.1 0.1 broadcast_in_dim.2.inv_base
  32.2 0.0 copy-done.3
  32.2 0.0 copy-done.5
  32.2 0.0 copy-done.8
  32.2 0.0 copy-done.10
  32.2 0.0 copy-start.6
  32.2 0.0 copy-start.11
  32.2 0.0 copy-start.12
  32.2 0.0 copy-start.13
  32.3 0.0 copy-start.14
  32.3 8.5 %inner.1 = (f32[8,8,32,128]{3,2,1,0:T(8,128)S(1)}, f32[4,2,8,8,128]{4,3,2,1,0:T(8,128)S(1)}, f32[2,32,128]{2,1,0:T(8,128)S(1)}) custom-call(s32[8,8]{1,0:T(8,128)S(1)} %copy-done.10, f32[8,8]{1,0:T(8,128)S(1)} %convert_divide_fusion.inv_lags, f32[256,128]{1,0:T(8,128)S(1)} %collective-permute-done.west, f32[256,128]{1,0:T(8,128)S(1)} %collective-permute-done.1.east, ...), custom_call_target="tpu_custom_call" | custom-call | flops 400000000 | bytes 30000000 | tf_op jit(solution)/shard_map/inner/pallas_call | solution.py:328
  40.8 0.0 collective-permute-done.3.south
  40.8 0.0 collective-permute-done.2.north
  40.8 0.0 copy-done.6
  40.8 0.0 copy-done.11
  40.8 0.0 copy-done.12
  40.9 0.0 copy-done.13
  40.9 0.0 copy-done.14
  40.9 12.5 %outer.1 = (f32[256,1024]{1,0:T(8,128)}, f32[1408,128]{1,0:T(8,128)S(1)}) custom-call(s32[8,8]{1,0:T(8,128)S(1)} %copy-done.10, f32[8,8]{1,0:T(8,128)S(1)} %convert_divide_fusion.inv_lags, s32[1,128]{1,0:T(1,128)S(1)} %copy-done.14, s32[2]{0:T(128)S(1)} %pad_add_fusion.lat, f32[256,1024]{1,0:T(8,128)S(1)} %copy-done.1, ...), custom_call_target="tpu_custom_call" | custom-call | flops 400000000 | bytes 20000000 | tf_op jit(solution)/shard_map/outer/pallas_call | solution.py:480
  53.4 24.4 %all_to_all.5 = f32[128,1,1408]{2,1,0:T(1,128)S(1)} all-to-all(f32[128,1,1408]{2,1,0:T(1,128)S(1)} %bitcast.8), channel_id=1, replica_groups=mesh['lat'=4,'lon'=32] {'lat','lon'}, dimensions={0} | all-to-all | bytes 1441792 | tf_op jit(solution)/shard_map/all_to_all | solution.py:577
  77.8 3.0 %cells.1 = (f32[8,512]{1,0:T(8,128)}, f32[1,512]{1,0:T(1,128)}) custom-call(f32[1408,128]{1,0:T(8,128)S(1)} %bitcast.7), custom_call_target="tpu_custom_call" | custom-call | tf_op jit(solution)/shard_map/cells/pallas_call | solution.py:531
  (6 shorter events, 0.0 us)
Async XLA Ops:
  2.3 21.2 %collective-permute-start.1 = (f32[256,128]{1,0:T(8,128)}, f32[256,128]{1,0:T(8,128)S(1)}, u32[]{:S(2)}, u32[]{:S(2)}) collective-permute-start(f32[256,128]{1,0:T(8,128)} %get-tuple-element.49), channel_id=1, source_target_pairs={{1,0},{2,1},{3,2},{4,3},{5,4},{6,5},{7,6},{8,7},{9,8},{10,9},{11,1... | collective-permute-start | bytes 393224 | tf_op jit(solution)/shard_map/ppermute | solution.py:549
  9.4 14.1 %collective-permute-start = (f32[256,128]{1,0:T(8,128)}, f32[256,128]{1,0:T(8,128)S(1)}, u32[]{:S(2)}, u32[]{:S(2)}) collective-permute-start(f32[256,128]{1,0:T(8,128)} %get-tuple-element.50), channel_id=1, source_target_pairs={{0,1},{1,2},{2,3},{3,4},{4,5},{5,6},{6,7},{7,8},{8,9},{9,10},{10,1... | collective-permute-start | bytes 393224 | tf_op jit(solution)/shard_map/ppermute | solution.py:548
  10.2 1.2 %copy-start = (f32[256,1024]{1,0:T(8,128)S(1)}, f32[256,1024]{1,0:T(8,128)}, u32[]{:S(2)}) copy-start(f32[256,1024]{1,0:T(8,128)} %own.3) | copy-start | bytes 3145732
  11.4 0.7 copy-start.9
  12.1 11.5 %copy-start.1 = (f32[256,1024]{1,0:T(8,128)S(1)}, f32[256,1024]{1,0:T(8,128)}, u32[]{:S(2)}) copy-start(f32[256,1024]{1,0:T(8,128)} %own.3) | copy-start | bytes 3145732
  17.4 1.0 %copy-start.2 = (f32[8,8,32,128]{3,2,1,0:T(8,128)}, f32[8,8,32,128]{3,2,1,0:T(8,128)S(1)}, u32[]{:S(2)}) copy-start(f32[8,8,32,128]{3,2,1,0:T(8,128)S(1)} %get-tuple-element.34.V_old) | copy-start | bytes 3145732
  18.4 1.0 %copy-start.4 = (f32[2,8,128,128]{3,2,1,0:T(8,128)}, f32[2,8,128,128]{3,2,1,0:T(8,128)S(1)}, u32[]{:S(2)}) copy-start(f32[2,8,128,128]{3,2,1,0:T(8,128)S(1)} %get-tuple-element.35.VT_old) | copy-start | bytes 3145732
  19.4 0.6 copy-start.7
  23.7 8.5 %copy-start.3 = (f32[8,8,32,128]{3,2,1,0:T(8,128)S(1)}, f32[8,8,32,128]{3,2,1,0:T(8,128)}, u32[]{:S(2)}) copy-start(f32[8,8,32,128]{3,2,1,0:T(8,128)} %copy-done.2) | copy-start | bytes 3145732
  23.7 8.5 %copy-start.5 = (f32[2,8,128,128]{3,2,1,0:T(8,128)S(1)}, f32[2,8,128,128]{3,2,1,0:T(8,128)}, u32[]{:S(2)}) copy-start(f32[2,8,128,128]{3,2,1,0:T(8,128)} %copy-done.4) | copy-start | bytes 3145732
  23.7 8.5 %copy-start.8 = (f32[2,128,128]{2,1,0:T(8,128)S(1)}, f32[2,128,128]{2,1,0:T(8,128)}, u32[]{:S(2)}) copy-start(f32[2,128,128]{2,1,0:T(8,128)} %copy-done.7) | copy-start | bytes 393220
  23.7 8.5 %copy-start.10 = (s32[8,8]{1,0:T(8,128)S(1)}, s32[8,8]{1,0:T(8,128)}, u32[]{:S(2)}) copy-start(s32[8,8]{1,0:T(8,128)} %lags.5) | copy-start | bytes 772
  23.8 17.0 %collective-permute-start.3 = (f32[128,1280]{1,0:T(8,128)S(1)}, f32[128,1280]{1,0:T(8,128)S(1)}, u32[]{:S(2)}, u32[]{:S(2)}) collective-permute-start(f32[128,1280]{1,0:T(8,128)S(1)} %get-tuple-element.47), channel_id=1, source_target_pairs={{32,0},{64,32},{96,64},{33,1},{65,33},{97,65},{34,2},{66,34},{98,6... | collective-permute-start | bytes 1966088 | tf_op jit(solution)/shard_map/ppermute | solution.py:564
  26.8 14.0 %collective-permute-start.2 = (f32[128,1280]{1,0:T(8,128)S(1)}, f32[128,1280]{1,0:T(8,128)S(1)}, u32[]{:S(2)}, u32[]{:S(2)}) collective-permute-start(f32[128,1280]{1,0:T(8,128)S(1)} %get-tuple-element.48), channel_id=1, source_target_pairs={{0,32},{32,64},{64,96},{1,33},{33,65},{65,97},{2,34},{34,66},{66,9... | collective-permute-start | bytes 1966088 | tf_op jit(solution)/shard_map/ppermute | solution.py:563
  32.2 8.6 %copy-start.6 = (f32[2,128,128]{2,1,0:T(8,128)S(1)}, f32[2,128,128]{2,1,0:T(8,128)}, u32[]{:S(2)}) copy-start(f32[2,128,128]{2,1,0:T(8,128)} %get-tuple-element.42.meta) | copy-start | bytes 393220
  32.2 8.6 %copy-start.11 = (s32[96,128]{1,0:T(8,128)S(1)}, s32[96,128]{1,0:T(8,128)}, u32[]{:S(2)}) copy-start(s32[96,128]{1,0:T(8,128)} %get-tuple-element.41.index) | copy-start | bytes 147460
  32.2 8.6 %copy-start.12 = (s32[4096,1]{0,1:T(1,128)S(1)}, s32[4096,1]{0,1:T(1,128)}, u32[]{:S(2)}) copy-start(s32[4096,1]{0,1:T(1,128)} %param.7) | copy-start | bytes 49156
  32.2 8.6 %copy-start.13 = (s32[4096]{0:T(1024)S(1)}, s32[4096]{0:T(1024)}, u32[]{:S(2)}) copy-start(s32[4096]{0:T(1024)} %param.9) | copy-start | bytes 49156
  32.3 8.6 %copy-start.14 = (s32[1,128]{1,0:T(1,128)S(1)}, s32[1,128]{1,0:T(1,128)}, u32[]{:S(2)}) copy-start(s32[1,128]{1,0:T(1,128)} %get-tuple-element.29.starts) | copy-start | bytes 1540

commit v4 on v2

--- a/solution.py
+++ b/solution.py
@@ -222,16 +222,31 @@
         c.wait()
 
 
+def one_of(flag, yes, no, sems, base):
+    @pl.when(flag)
+    def _():
+        for i, (a, b) in enumerate(yes):
+            pltpu.make_async_copy(a, b, sems.at[base + i]).start()
+
+    @pl.when(jnp.logical_not(flag))
+    def _():
+        for i, (a, b) in enumerate(no):
+            pltpu.make_async_copy(a, b, sems.at[base + i]).start()
+
+    return [pltpu.make_async_copy(a, b, sems.at[base + i]) for i, (a, b) in enumerate(yes)]
+
+
 def cols(j):
     return pl.ds(j * 128, 128)
 
 
 def inner_kernel(
-    lags, inv_lags, own, west, east, inv_base, inv_row, V_ref, S_ref, pooled_ref, Hn, H, Tn, T, VT, ST, X, Xn, rise, sems
+    lags, inv_lags, place, own, near, far, inv_base, inv_row, V_ref, S_ref, pooled_ref, Hn, H, Tn, T, VT, ST, X, Xn, rise, sems
 ):
-    copies(
-        [(own.at[:, cols(j)], Hn.at[1 + j]) for j in range(8)] + [(west, Hn.at[0]), (east, Hn.at[9])], sems
-    )
+    sides = one_of(place[2] == 1, ((near, Hn.at[0]), (far, Hn.at[9])), ((far, Hn.at[0]), (near, Hn.at[9])), sems, 8)
+    copies([(own.at[:, cols(j)], Hn.at[1 + j]) for j in range(8)], sems)
+    for c in sides:
+        c.wait()
     for c in range(10):
         for p in range(8):
             H[c, p] = Hn[c, pl.ds(p, 32, stride=8), :]
@@ -282,7 +297,7 @@
             jax.ShapeDtypeStruct((4, 3, 8, 8, 128), F32),
             jax.ShapeDtypeStruct((2, NBR, 128), F32),
         ),
-        in_specs=[SMEM] * 2 + [ANY] * 3 + [VMEM] * 2,
+        in_specs=[SMEM] * 3 + [ANY] * 3 + [VMEM] * 2,
         out_specs=[VMEM] * 3,
         scratch_shapes=[
             pltpu.VMEM((10, 256, 128), F32),
@@ -302,21 +317,28 @@
 
 
 def outer_kernel(
-    lags, inv_lags, starts, lat, own, north, south, west, east, inv_base, V_in, S_in, pooled, weight, owner, index, meta,
+    lags, inv_lags, starts, place, own, same, other, near, far, inv_base, V_in, S_in, pooled, weight, owner, index, meta,
     svf_ref, out_ref, Hn, H, S, V, Vn, R, Z, Y, O, acc, rise, sems,
 ):
-    pairs = [(own.at[:, cols(j)], Hn.at[1 + j, pl.ds(128, 256)]) for j in range(8)]
-    pairs += [(west, Hn.at[0, pl.ds(128, 256)]), (east, Hn.at[9, pl.ds(128, 256)])]
-    pairs += [(north.at[:, cols(j)], Hn.at[j, pl.ds(0, 128)]) for j in range(10)]
-    pairs += [(south.at[:, cols(j)], Hn.at[j, pl.ds(384, 128)]) for j in range(10)]
-    copies(pairs, sems)
-
-    @pl.when(lat[0] == 0)
+    def rows(ref, first):
+        return [(ref.at[:, cols(j)], Hn.at[j, pl.ds(first, 128)]) for j in range(10)]
+
+    def side(ref, c):
+        return (ref, Hn.at[c, pl.ds(128, 256)])
+
+    made = one_of(place[2] == 1, (side(near, 0), side(far, 9)), (side(far, 0), side(near, 9)), sems, 8)
+    odd = lax.bitwise_and(place[0], 1) == 1
+    made += one_of(odd, rows(same, 0) + rows(other, 384), rows(other, 0) + rows(same, 384), sems, 10)
+    copies([(own.at[:, cols(j)], Hn.at[1 + j, pl.ds(128, 256)]) for j in range(8)], sems)
+    for c in made:
+        c.wait()
+
+    @pl.when(place[0] == 0)
     def _():
         for c in range(10):
             Hn[c, 0:128, :] = jnp.broadcast_to(Hn[c, 128:129, :], (128, 128))
 
-    @pl.when(lat[0] == lat[1] - 1)
+    @pl.when(place[0] == place[1] - 1)
     def _():
         for c in range(10):
             Hn[c, 384:512, :] = jnp.broadcast_to(Hn[c, 383:384, :], (128, 128))
@@ -466,7 +488,7 @@
         hot = (low == jnp.broadcast_to(cell - 128.0 * upper, (128, 512)).astype(BF16)).astype(BF16)
         return acc + lax.dot_general(jnp.concatenate(left, axis=0), hot, NT, preferred_element_type=F32)
 
-    acc = lax.fori_loop(0, N_DEV // 4, accumulate, jnp.zeros((128, 128), F32), unroll=8)
+    acc = lax.fori_loop(0, N_DEV // 4, accumulate, jnp.zeros((128, 128), F32), unroll=True)
     sums = jnp.concatenate([acc[h * 32 : h * 32 + 16] + acc[h * 32 + 16 : h * 32 + 32] for h in range(4)], axis=1)
     area = jnp.maximum(sums[15:16, :] * (1.0 / 64.0), 1.0)
     horizon_ref[...] = sums[0:8] / area
@@ -490,17 +512,32 @@
     n_lon = lax.axis_size("lon")
     W = FARTHEST_LAG
     own = terrain_surface
-    east_pairs = [((i + 1) % n_lon, i) for i in range(n_lon)]
-    west = lax.ppermute(own[:, width - W :], "lon", [(j, i) for i, j in east_pairs])
-    east = lax.ppermute(own[:, :W], "lon", east_pairs)
+    lat, lon = lax.axis_index("lat"), lax.axis_index("lon")
+    odd = lon % 2
+
+    def exchange(block, axis, size, first, wrap):
+        pairs = []
+        for i in range(first, size, 2):
+            if i + 1 < size or wrap:
+                pairs += [(i, (i + 1) % size), ((i + 1) % size, i)]
+        return lax.ppermute(block, axis, pairs)
+
+    def edge(block, at_end, dim):
+        return lax.dynamic_slice_in_dim(block, jnp.where(at_end, block.shape[dim] - W, 0), W, axis=dim)
+
+    far = exchange(edge(own, odd == 1, 1), "lon", n_lon, 1, True)
+    near = exchange(edge(own, odd == 0, 1), "lon", n_lon, 0, True)
     weight = footprint_weight.reshape(NBR, 128)
     owner = holder_devices.reshape(NBR, 128)
     start, index, meta = route(owner, holder_region_slot.reshape(NBR, 128), weight)
-    west, east, start, index, meta = lax.optimization_barrier((west, east, start, index, meta))
-    wide = jnp.concatenate([west, own, east], axis=1)
-    down = [(i, i + 1) for i in range(n_lat - 1)]
-    north = lax.ppermute(wide[rows - W :], "lat", down)
-    south = lax.ppermute(wide[:W], "lat", [(j, i) for i, j in down])
+    near, far, start, index, meta = lax.optimization_barrier((near, far, start, index, meta))
+    west, east = jnp.where(odd == 1, near, far), jnp.where(odd == 1, far, near)
+
+    def wide(at_end):
+        return jnp.concatenate([edge(west, at_end, 0), edge(own, at_end, 0), edge(east, at_end, 0)], axis=1)
+
+    other = exchange(wide(lat % 2 == 1), "lat", n_lat, 1, False)
+    same = exchange(wide(lat % 2 == 0), "lat", n_lat, 0, False)
 
     rows_global = (lax.axis_index("lat") * rows + jnp.arange(rows, dtype=jnp.int32)).astype(F32)
     latitude = 47.0 - (rows_global + 0.5) / 1200.0
@@ -509,11 +546,11 @@
     inv_row = (1.0 / jnp.sqrt(across)).reshape(2, 128)
     inv_base = 1.0 / jnp.sqrt(pixel_size**2 + across)
     inv_base = jnp.broadcast_to(inv_base.reshape(32, 8).T[:, :, None], (8, 32, 128))
-    lat = jnp.stack([lax.axis_index("lat").astype(jnp.int32), jnp.int32(n_lat)])
+    place = jnp.stack([lat.astype(jnp.int32), jnp.int32(n_lat), odd.astype(jnp.int32)])
     inv_lags = 1.0 / azimuth_lag_tallies.astype(F32)
-    part, sums, pooled = inner(azimuth_lag_tallies, inv_lags, own, west, east, inv_base, inv_row)
+    part, sums, pooled = inner(azimuth_lag_tallies, inv_lags, place, own, near, far, inv_base, inv_row)
     fine_svf, packed = outer(
-        azimuth_lag_tallies, inv_lags, start, lat, own, north, south, west, east, inv_base, part, sums, pooled,
+        azimuth_lag_tallies, inv_lags, start, place, own, same, other, near, far, inv_base, part, sums, pooled,
         weight, owner, index, meta,
     )
     packed = packed.reshape(N_DEV, 1, 11 * 128)

time: 73.1 us -> 70.7 us (0.967)
  starting transfers between devices: 16.4 us -> 12.9 us
  blocking collectives: 17.6 us -> 19.4 us
  waiting for transfers between devices: 4.51 us -> 3.12 us
  other arithmetic: 0.19 us -> 1.14 us
    ppermute x4, starting transfers between devices: 16.4 us -> 12.9 us  [exchange(): return lax.ppermute(block, axis, pairs)]
    slice x2 -> x0, local copies, waits for them, and re-layouts: 2 us -> none  [the longest x1 1.08 us: shards(): east = lax.ppermute(own[:, :W], 'lon', east_pairs)]
    all_to_all x1, blocking collectives: 17.6 us -> 19.4 us  [shards(): lax.all_to_all(packed, ('lat', 'lon'), split_axis=0, concat_axis=0, tiled...]
    ppermute x4, waiting for transfers between devices: 4.51 us -> 3.12 us  [exchange(): return lax.ppermute(block, axis, pairs)]
    dynamic_slice x0 -> x3, local copies, waits for them, and re-layouts: none -> 1.2 us  [edge(): lax.dynamic_slice_in_dim(block, jnp.where(at_end, block.shape[dim] - W, 0...]
    unnamed x16 -> x14, local copies, waits for them, and re-layouts: 0.12 us -> 1.12 us
    concatenate x0 -> x2, other arithmetic: none -> 0.93 us  [wide(): jnp.concatenate([edge(west, at_end, 0), edge(own, at_end, 0), edge(east,...]
  transfers between devices with their start and end apart: 4 -> 4, of which waited for: 1 -> 1; matrix products, arithmetic and copies ran while one was open for 0% -> 2% of each run, Pallas kernels for 21% -> 22%
where the time goes in v4:
time: 70.7 us; the launch traced here: 70.4 us
  Pallas kernels  30.6 us (43%)
  blocking collectives  19.4 us (27%)
  starting transfers between devices  12.9 us (18%)
  waiting for transfers between devices  3.12 us (4%)
  local copies, waits for them, and re-layouts  2.42 us (3%)
  other arithmetic  1.14 us (2%)
  between operations  0.84 us (1%)
    all_to_all x1, blocking collectives, shards(): lax.all_to_all(packed, ('lat', 'lon'), split_axis=0, concat_axis=0, tiled...  19.4 us
    ppermute x4, starting transfers between devices, exchange(): return lax.ppermute(block, axis, pairs)  12.9 us
    pallas_call x1, Pallas kernels, outer(): pl.pallas_call(outer_kernel, name='outer', out_shape=(jax.ShapeDtypeStruc...  12.5 us
    pallas_call x1, Pallas kernels, inner(): pl.pallas_call(inner_kernel, name='inner', out_shape=(jax.ShapeDtypeStruc...  12 us
    pallas_call x1, Pallas kernels, route(): pl.pallas_call(route_kernel, name='route', out_shape=(jax.ShapeDtypeStruc...  3.53 us
    ppermute x4, waiting for transfers between devices, exchange(): return lax.ppermute(block, axis, pairs)  3.12 us
    pallas_call x1, Pallas kernels, cells(): pl.pallas_call(cells_kernel, name='cells', out_shape=(jax.ShapeDtypeStruc...  2.55 us
  transfers between devices with their start and end apart: 4, of which 1 were waited for; matrix products, arithmetic and copies ran while one was open for 2% of the time, Pallas kernels for 22%

profile of v4, /device:TPU:1, one launch (start us, length us, event | category | flops | bytes accessed | tf_op | source)
XLA Modules:
  0.0 70.4 jit_solution(8598842147300841212)
XLA Ops:
  0.6 0.0 copy-start
  0.7 1.1 %constant_dynamic-slice_fusion.6 = (f32[256,128]{1,0:T(8,128)S(1)}, f32[256,128]{1,0:T(8,128)S(1)}) fusion(f32[256,1024]{1,0:T(8,128)} %own.3, s32[]{:T(128)S(6)} %select_n.52, s32[]{:T(128)S(6)} %select_n.51), kind=kLoop, calls=%fused_computation.12 | loop fusion | bytes 524296 | tf_op jit(solution)/shard_map/dynamic_slice | solution.py:526
  1.7 7.2 %collective-permute-start.1 = (f32[256,128]{1,0:T(8,128)S(1)}, f32[256,128]{1,0:T(8,128)S(1)}, u32[]{:S(2)}, u32[]{:S(2)}) collective-permute-start(f32[256,128]{1,0:T(8,128)S(1)} %get-tuple-element.35), channel_id=1, source_target_pairs={{1,2},{2,1},{3,4},{4,3},{5,6},{6,5},{7,8},{8,7},{9,10},{10,9},{11,... | collective-permute-start | bytes 393224 | tf_op jit(solution)/shard_map/ppermute | solution.py:523
  8.9 0.0 collective-permute-start
  8.9 3.5 %route.1 = (s32[1,128]{1,0:T(1,128)}, s32[96,128]{1,0:T(8,128)}, f32[2,128,128]{2,1,0:T(8,128)}) custom-call(s32[32,128]{1,0:T(8,128)} %bitcast.10, s32[32,128]{1,0:T(8,128)} %bitcast.14, s32[32,128]{1,0:T(8,128)} %bitcast.12), custom_call_target="tpu_custom_call" | custom-call | flops 400000000 | bytes 200000 | tf_op jit(solution)/shard_map/route/pallas_call | solution.py:87
  12.5 0.0 copy-done
  12.5 0.1 constant_dynamic-slice_fusion.1
  12.6 0.0 collective-permute-done.1.far
  12.6 3.1 %collective-permute-done.near = f32[256,128]{1,0:T(8,128)S(1)} collective-permute-done((f32[256,128]{1,0:T(8,128)S(1)}, f32[256,128]{1,0:T(8,128)S(1)}, u32[]{:S(2)}, u32[]{:S(2)}) %collective-permute-start) | collective-permute-done | bytes 131104 | tf_op jit(solution)/shard_map/ppermute | solution.py:523
  15.8 0.6 collective-permute-start.2
  16.4 0.9 %pad_maximum_fusion.1 = f32[128,1280]{1,0:T(8,128)} fusion(f32[128,128]{1,0:T(8,128)S(1)} %get-tuple-element.41, f32[128,1024]{1,0:T(8,128)S(1)} %get-tuple-element.33, f32[128,128]{1,0:T(8,128)S(1)} %get-tuple-element.44), kind=kLoop, calls=%fused_computation.1 | loop fusion | flops 327680 | bytes 1310720 | tf_op jit(solution)/shard_map/concatenate | solution.py:537
  17.3 5.1 %collective-permute-start.3 = (f32[128,1280]{1,0:T(8,128)}, f32[128,1280]{1,0:T(8,128)S(1)}, u32[]{:S(2)}, u32[]{:S(2)}) collective-permute-start(f32[128,1280]{1,0:T(8,128)} %pad_maximum_fusion.1), channel_id=1, source_target_pairs={{32,64},{64,32},{33,65},{65,33},{34,66},{66,34},{35,67},{67,35},{3... | collective-permute-start | bytes 1966088 | tf_op jit(solution)/shard_map/ppermute | solution.py:523
  22.4 0.0 copy-start.5
  22.4 0.1 pad_add_fusion.place
  22.5 0.1 multiply_rsqrt_fusion.inv_row
  22.5 0.1 add_rsqrt_fusion
  22.6 0.5 copy-done.5
  23.1 0.1 broadcast_in_dim.2.inv_base
  23.2 0.0 copy-start.1
  23.2 0.0 copy-start.2
  23.2 0.0 copy-start.3
  23.2 0.0 copy-start.4
  23.2 12.0 %inner.1 = (f32[8,8,32,128]{3,2,1,0:T(8,128)S(1)}, f32[4,3,8,8,128]{4,3,2,1,0:T(8,128)S(1)}, f32[2,32,128]{2,1,0:T(8,128)S(1)}) custom-call(s32[8,8]{1,0:T(8,128)S(1)} %copy-done.5, f32[8,8]{1,0:T(8,128)S(1)} %convert_divide_fusion.inv_lags, s32[3]{0:T(128)S(1)} %pad_add_fusion.place, f32[256,1024]{1,0:T(8,128)S(1)} %copy-done, ...), custom_call_target="tpu_custom_call" | custom-call | flops 400000000 | bytes 30000000 | tf_op jit(solution)/shard_map/inner/pallas_call | solution.py:292
  35.3 0.0 collective-permute-done.2.same
  35.3 0.0 collective-permute-done.3.other
  35.3 0.0 copy-start.6
  35.3 0.0 copy-done.1
  35.3 0.0 copy-done.2
  35.3 0.0 copy-done.3
  35.3 0.0 copy-done.4
  35.3 0.6 copy-done.6
  35.9 12.5 %outer.1 = (f32[256,1024]{1,0:T(8,128)}, f32[1408,128]{1,0:T(8,128)S(1)}) custom-call(s32[8,8]{1,0:T(8,128)S(1)} %copy-done.5, f32[8,8]{1,0:T(8,128)S(1)} %convert_divide_fusion.inv_lags, s32[1,128]{1,0:T(1,128)S(1)} %copy-done.6, s32[3]{0:T(128)S(1)} %pad_add_fusion.place, f32[256,1024]{1,0:T(8,128)S(1)} %copy-done, ...), custom_call_target="tpu_custom_call" | custom-call | flops 400000000 | bytes 20000000 | tf_op jit(solution)/shard_map/outer/pallas_call | solution.py:448
  48.4 19.4 %all_to_all.5 = f32[128,1,1408]{2,1,0:T(1,128)S(1)} all-to-all(f32[128,1,1408]{2,1,0:T(1,128)S(1)} %bitcast.9), channel_id=1, replica_groups=mesh['lat'=4,'lon'=32] {'lat','lon'}, dimensions={0} | all-to-all | bytes 1441792 | tf_op jit(solution)/shard_map/all_to_all | solution.py:557
  67.8 2.6 %cells.1 = (f32[8,512]{1,0:T(8,128)}, f32[1,512]{1,0:T(1,128)}) custom-call(f32[1408,128]{1,0:T(8,128)S(1)} %bitcast.8), custom_call_target="tpu_custom_call" | custom-call | tf_op jit(solution)/shard_map/cells/pallas_call | solution.py:499
  (4 shorter events, 0.1 us)
Async XLA Ops:
  0.6 11.8 %copy-start = (f32[256,1024]{1,0:T(8,128)S(1)}, f32[256,1024]{1,0:T(8,128)}, u32[]{:S(2)}) copy-start(f32[256,1024]{1,0:T(8,128)} %own.3) | copy-start | bytes 3145732
  1.7 10.8 %collective-permute-start.1 = (f32[256,128]{1,0:T(8,128)S(1)}, f32[256,128]{1,0:T(8,128)S(1)}, u32[]{:S(2)}, u32[]{:S(2)}) collective-permute-start(f32[256,128]{1,0:T(8,128)S(1)} %get-tuple-element.35), channel_id=1, source_target_pairs={{1,2},{2,1},{3,4},{4,3},{5,6},{6,5},{7,8},{8,7},{9,10},{10,9},{11,... | collective-permute-start | bytes 393224 | tf_op jit(solution)/shard_map/ppermute | solution.py:523
  8.9 6.8 %collective-permute-start = (f32[256,128]{1,0:T(8,128)S(1)}, f32[256,128]{1,0:T(8,128)S(1)}, u32[]{:S(2)}, u32[]{:S(2)}) collective-permute-start(f32[256,128]{1,0:T(8,128)S(1)} %get-tuple-element.36), channel_id=1, source_target_pairs={{0,1},{1,0},{2,3},{3,2},{4,5},{5,4},{6,7},{7,6},{8,9},{9,8},{10,11... | collective-permute-start | bytes 393224 | tf_op jit(solution)/shard_map/ppermute | solution.py:523
  15.8 19.5 %collective-permute-start.2 = (f32[128,1280]{1,0:T(8,128)S(1)}, f32[128,1280]{1,0:T(8,128)S(1)}, u32[]{:S(2)}, u32[]{:S(2)}) collective-permute-start(f32[128,1280]{1,0:T(8,128)S(1)} %pad_maximum_fusion), channel_id=1, source_target_pairs={{0,32},{32,0},{64,96},{96,64},{1,33},{33,1},{65,97},{97,65},{2,34}... | collective-permute-start | bytes 1966088 | tf_op jit(solution)/shard_map/ppermute | solution.py:523
  17.3 18.0 %collective-permute-start.3 = (f32[128,1280]{1,0:T(8,128)}, f32[128,1280]{1,0:T(8,128)S(1)}, u32[]{:S(2)}, u32[]{:S(2)}) collective-permute-start(f32[128,1280]{1,0:T(8,128)} %pad_maximum_fusion.1), channel_id=1, source_target_pairs={{32,64},{64,32},{33,65},{65,33},{34,66},{66,34},{35,67},{67,35},{3... | collective-permute-start | bytes 1966088 | tf_op jit(solution)/shard_map/ppermute | solution.py:523
  22.4 0.7 copy-start.5
  23.2 12.1 %copy-start.1 = (f32[2,128,128]{2,1,0:T(8,128)S(1)}, f32[2,128,128]{2,1,0:T(8,128)}, u32[]{:S(2)}) copy-start(f32[2,128,128]{2,1,0:T(8,128)} %get-tuple-element.28.meta) | copy-start | bytes 393220
  23.2 12.1 %copy-start.2 = (s32[96,128]{1,0:T(8,128)S(1)}, s32[96,128]{1,0:T(8,128)}, u32[]{:S(2)}) copy-start(s32[96,128]{1,0:T(8,128)} %get-tuple-element.27.index) | copy-start | bytes 147460
  23.2 12.1 %copy-start.3 = (s32[4096,1]{0,1:T(1,128)S(1)}, s32[4096,1]{0,1:T(1,128)}, u32[]{:S(2)}) copy-start(s32[4096,1]{0,1:T(1,128)} %param.7) | copy-start | bytes 49156
  23.2 12.1 %copy-start.4 = (s32[4096]{0:T(1024)S(1)}, s32[4096]{0:T(1024)}, u32[]{:S(2)}) copy-start(s32[4096]{0:T(1024)} %param.9) | copy-start | bytes 49156
  35.3 0.7 copy-start.6

commit v5 on v4

--- a/solution.py
+++ b/solution.py
@@ -95,6 +95,7 @@
         in_specs=[VMEM] * 3,
         out_specs=[VMEM] * 3,
         scratch_shapes=[pltpu.VMEM((NBR, 128), F32)],
+        compiler_params=pltpu.CompilerParams(vmem_limit_bytes=8 * 1024 * 1024),
         cost_estimate=pl.CostEstimate(flops=int(4e8), bytes_accessed=200000, transcendentals=0),
     )(owner, slot, weight)
 
@@ -311,7 +312,7 @@
             pltpu.VMEM((3, 2, 4, 8, 8, 128), F32),
             pltpu.SemaphoreType.DMA((10,)),
         ],
-        compiler_params=pltpu.CompilerParams(vmem_limit_bytes=32 * 1024 * 1024),
+        compiler_params=pltpu.CompilerParams(vmem_limit_bytes=20 * 1024 * 1024),
         cost_estimate=pl.CostEstimate(flops=int(4e8), bytes_accessed=30000000, transcendentals=0),
     )(*args)
 
@@ -465,7 +466,7 @@
             pltpu.VMEM((2, 2, 4, 8, 8, 128), F32),
             pltpu.SemaphoreType.DMA((38,)),
         ],
-        compiler_params=pltpu.CompilerParams(vmem_limit_bytes=32 * 1024 * 1024),
+        compiler_params=pltpu.CompilerParams(vmem_limit_bytes=20 * 1024 * 1024),
         cost_estimate=pl.CostEstimate(flops=int(4e8), bytes_accessed=20000000, transcendentals=0),
     )(*args)
 
@@ -502,7 +503,7 @@
         out_shape=(jax.ShapeDtypeStruct((AZ, CELLS_DEV), F32), jax.ShapeDtypeStruct((1, CELLS_DEV), F32)),
         in_specs=[VMEM],
         out_specs=[VMEM] * 2,
-        compiler_params=pltpu.CompilerParams(vmem_limit_bytes=24 * 1024 * 1024),
+        compiler_params=pltpu.CompilerParams(vmem_limit_bytes=8 * 1024 * 1024),
     )(got)
 
 
@@ -530,7 +531,8 @@
     weight = footprint_weight.reshape(NBR, 128)
     owner = holder_devices.reshape(NBR, 128)
     start, index, meta = route(owner, holder_region_slot.reshape(NBR, 128), weight)
-    near, far, start, index, meta = lax.optimization_barrier((near, far, start, index, meta))
+    inv_lags = 1.0 / azimuth_lag_tallies.astype(F32)
+    near, far, start, inv_lags = lax.optimization_barrier((near, far, start, inv_lags))
     west, east = jnp.where(odd == 1, near, far), jnp.where(odd == 1, far, near)
 
     def wide(at_end):
@@ -547,7 +549,6 @@
     inv_base = 1.0 / jnp.sqrt(pixel_size**2 + across)
     inv_base = jnp.broadcast_to(inv_base.reshape(32, 8).T[:, :, None], (8, 32, 128))
     place = jnp.stack([lat.astype(jnp.int32), jnp.int32(n_lat), odd.astype(jnp.int32)])
-    inv_lags = 1.0 / azimuth_lag_tallies.astype(F32)
     part, sums, pooled = inner(azimuth_lag_tallies, inv_lags, place, own, near, far, inv_base, inv_row)
     fine_svf, packed = outer(
         azimuth_lag_tallies, inv_lags, start, place, own, same, other, near, far, inv_base, part, sums, pooled,

time: 70.7 us -> 70.3 us (level)
  local copies, waits for them, and re-layouts: 2.42 us -> 4.06 us
  Pallas kernels: 30.6 us -> 29.1 us
  waiting for transfers between devices: 3.12 us -> 1.67 us
    unnamed x14, local copies, waits for them, and re-layouts: 1.12 us -> 2.76 us
    ppermute x4, waiting for transfers between devices: 3.12 us -> 1.67 us  [exchange(): return lax.ppermute(block, axis, pairs)]
    pallas_call x1, Pallas kernels: 3.53 us -> 2.11 us  [route(): pl.pallas_call(route_kernel, name='route', out_shape=(jax.ShapeDtypeStruc...]
  transfers between devices with their start and end apart: 4 -> 4, of which waited for: 1 -> 1; matrix products, arithmetic and copies ran while one was open for 2% -> 3% of each run, Pallas kernels for 22% -> 20%
where the time goes in v5:
time: 70.3 us; the launch traced here: 69.7 us
  Pallas kernels  29.1 us (41%)
  blocking collectives  19.4 us (28%)
  starting transfers between devices  12.9 us (18%)
  local copies, waits for them, and re-layouts  4.06 us (6%)
  other arithmetic  1.82 us (3%)
  waiting for transfers between devices  1.67 us (2%)
  between operations  0.8 us (1%)
    all_to_all x1, blocking collectives, shards(): lax.all_to_all(packed, ('lat', 'lon'), split_axis=0, concat_axis=0, tiled...  19.4 us
    ppermute x4, starting transfers between devices, exchange(): return lax.ppermute(block, axis, pairs)  12.9 us
    pallas_call x1, Pallas kernels, outer(): pl.pallas_call(outer_kernel, name='outer', out_shape=(jax.ShapeDtypeStruc...  12.4 us
    pallas_call x1, Pallas kernels, inner(): pl.pallas_call(inner_kernel, name='inner', out_shape=(jax.ShapeDtypeStruc...  12 us
    unnamed x14, local copies, waits for them, and re-layouts  2.76 us
    pallas_call x1, Pallas kernels, cells(): pl.pallas_call(cells_kernel, name='cells', out_shape=(jax.ShapeDtypeStruc...  2.55 us
    pallas_call x1, Pallas kernels, route(): pl.pallas_call(route_kernel, name='route', out_shape=(jax.ShapeDtypeStruc...  2.11 us
    ppermute x4, waiting for transfers between devices, exchange(): return lax.ppermute(block, axis, pairs)  1.67 us
  transfers between devices with their start and end apart: 4, of which 1 were waited for; matrix products, arithmetic and copies ran while one was open for 3% of the time, Pallas kernels for 20%

profile of v5, /device:TPU:1, one launch (start us, length us, event | category | flops | bytes accessed | tf_op | source)
XLA Modules:
  0.0 69.7 jit_solution(346432924030973913)
XLA Ops:
  0.6 0.0 copy-start
  0.7 1.1 %constant_dynamic-slice_fusion.6 = (f32[256,128]{1,0:T(8,128)S(1)}, f32[256,128]{1,0:T(8,128)S(1)}) fusion(f32[256,1024]{1,0:T(8,128)} %own.3, s32[]{:T(128)S(6)} %select_n.52, s32[]{:T(128)S(6)} %select_n.51), kind=kLoop, calls=%fused_computation.12 | loop fusion | bytes 524296 | tf_op jit(solution)/shard_map/dynamic_slice | solution.py:527
  1.7 7.2 %collective-permute-start.1 = (f32[256,128]{1,0:T(8,128)S(1)}, f32[256,128]{1,0:T(8,128)S(1)}, u32[]{:S(2)}, u32[]{:S(2)}) collective-permute-start(f32[256,128]{1,0:T(8,128)S(1)} %get-tuple-element.33), channel_id=1, source_target_pairs={{1,2},{2,1},{3,4},{4,3},{5,6},{6,5},{7,8},{8,7},{9,10},{10,9},{11,... | collective-permute-start | bytes 393224 | tf_op jit(solution)/shard_map/ppermute | solution.py:524
  8.9 0.0 collective-permute-start
  8.9 0.7 convert_divide_fusion.inv_lags
  9.6 0.0 copy-start.1
  9.6 0.7 %copy-done.1 = s32[4096,1]{0,1:T(1,128)S(1)} copy-done((s32[4096,1]{0,1:T(1,128)S(1)}, s32[4096,1]{0,1:T(1,128)}, u32[]{:S(2)}) %copy-start.1) | copy-done | bytes 16408
  10.3 0.0 copy-start.3
  10.3 0.7 %copy-done.3 = s32[4096]{0:T(1024)S(1)} copy-done((s32[4096]{0:T(1024)S(1)}, s32[4096]{0:T(1024)}, u32[]{:S(2)}) %copy-start.3) | copy-done | bytes 16408
  11.1 0.0 copy-start.6
  11.1 0.7 %copy-done.6 = s32[4096]{0:T(1024)S(1)} copy-done((s32[4096]{0:T(1024)S(1)}, s32[4096]{0:T(1024)}, u32[]{:S(2)}) %copy-start.6) | copy-done | bytes 16408
  11.8 2.1 %route.1 = (s32[1,128]{1,0:T(1,128)S(1)}, s32[96,128]{1,0:T(8,128)S(1)}, f32[2,128,128]{2,1,0:T(8,128)S(1)}) custom-call(s32[32,128]{1,0:T(8,128)S(1)} %bitcast.10, s32[32,128]{1,0:T(8,128)S(1)} %bitcast.14, s32[32,128]{1,0:T(8,128)S(1)} %bitcast.12), custom_call_target="tpu_custom_call" | custom-call | flops 400000000 | bytes 200000 | tf_op jit(solution)/shard_map/route/pallas_call | solution.py:87
  13.9 0.0 copy-done
  13.9 0.1 constant_dynamic-slice_fusion.1
  14.0 0.0 collective-permute-done.1.far
  14.0 1.7 %collective-permute-done.near = f32[256,128]{1,0:T(8,128)S(1)} collective-permute-done((f32[256,128]{1,0:T(8,128)S(1)}, f32[256,128]{1,0:T(8,128)S(1)}, u32[]{:S(2)}, u32[]{:S(2)}) %collective-permute-start) | collective-permute-done | bytes 131104 | tf_op jit(solution)/shard_map/ppermute | solution.py:524
  15.8 0.6 collective-permute-start.2
  16.4 0.9 %pad_maximum_fusion.1 = f32[128,1280]{1,0:T(8,128)} fusion(f32[128,128]{1,0:T(8,128)S(1)} %get-tuple-element.39, f32[128,1024]{1,0:T(8,128)S(1)} %get-tuple-element.31, f32[128,128]{1,0:T(8,128)S(1)} %get-tuple-element.42), kind=kLoop, calls=%fused_computation.1 | loop fusion | flops 327680 | bytes 1310720 | tf_op jit(solution)/shard_map/concatenate | solution.py:539
  17.3 5.1 %collective-permute-start.3 = (f32[128,1280]{1,0:T(8,128)}, f32[128,1280]{1,0:T(8,128)S(1)}, u32[]{:S(2)}, u32[]{:S(2)}) collective-permute-start(f32[128,1280]{1,0:T(8,128)} %pad_maximum_fusion.1), channel_id=1, source_target_pairs={{32,64},{64,32},{33,65},{65,33},{34,66},{66,34},{35,67},{67,35},{3... | collective-permute-start | bytes 1966088 | tf_op jit(solution)/shard_map/ppermute | solution.py:524
  22.4 0.1 pad_add_fusion.place
  22.5 0.1 multiply_rsqrt_fusion.inv_row
  22.5 0.1 add_rsqrt_fusion
  22.6 0.0 copy-start.5
  22.6 0.1 broadcast_in_dim.2.inv_base
  22.7 0.6 copy-done.5
  23.3 0.0 copy-start.2
  23.3 0.0 copy-start.4
  23.3 12.0 %inner.1 = (f32[8,8,32,128]{3,2,1,0:T(8,128)S(1)}, f32[4,3,8,8,128]{4,3,2,1,0:T(8,128)S(1)}, f32[2,32,128]{2,1,0:T(8,128)S(1)}) custom-call(s32[8,8]{1,0:T(8,128)S(1)} %copy-done.5, f32[8,8]{1,0:T(8,128)S(1)} %convert_divide_fusion.inv_lags, s32[3]{0:T(128)S(1)} %pad_add_fusion.place, f32[256,1024]{1,0:T(8,128)S(1)} %copy-done, ...), custom_call_target="tpu_custom_call" | custom-call | flops 400000000 | bytes 30000000 | tf_op jit(solution)/shard_map/inner/pallas_call | solution.py:293
  35.3 0.0 collective-permute-done.2.same
  35.3 0.0 collective-permute-done.3.other
  35.3 0.0 copy-done.2
  35.4 0.0 copy-done.4
  35.4 12.4 %outer.1 = (f32[256,1024]{1,0:T(8,128)}, f32[1408,128]{1,0:T(8,128)S(1)}) custom-call(s32[8,8]{1,0:T(8,128)S(1)} %copy-done.5, f32[8,8]{1,0:T(8,128)S(1)} %convert_divide_fusion.inv_lags, s32[1,128]{1,0:T(1,128)S(1)} %get-tuple-element.19.starts, s32[3]{0:T(128)S(1)} %pad_add_fusion.place, f32[256,1024]{1,0:T(8,128)S(1)} %copy-done, ...), custom_call_target="tpu_custom_call" | custom-call | flops 400000000 | bytes 20000000 | tf_op jit(solution)/shard_map/outer/pallas_call | solution.py:449
  47.8 19.4 %all_to_all.5 = f32[128,1,1408]{2,1,0:T(1,128)S(1)} all-to-all(f32[128,1,1408]{2,1,0:T(1,128)S(1)} %bitcast.9), channel_id=1, replica_groups=mesh['lat'=4,'lon'=32] {'lat','lon'}, dimensions={0} | all-to-all | bytes 1441792 | tf_op jit(solution)/shard_map/all_to_all | solution.py:558
  67.2 2.6 %cells.1 = (f32[8,512]{1,0:T(8,128)}, f32[1,512]{1,0:T(1,128)}) custom-call(f32[1408,128]{1,0:T(8,128)S(1)} %bitcast.8), custom_call_target="tpu_custom_call" | custom-call | tf_op jit(solution)/shard_map/cells/pallas_call | solution.py:500
  (3 shorter events, 0.1 us)
Async XLA Ops:
  0.6 13.3 %copy-start = (f32[256,1024]{1,0:T(8,128)S(1)}, f32[256,1024]{1,0:T(8,128)}, u32[]{:S(2)}) copy-start(f32[256,1024]{1,0:T(8,128)} %own.3) | copy-start | bytes 3145732
  1.7 12.3 %collective-permute-start.1 = (f32[256,128]{1,0:T(8,128)S(1)}, f32[256,128]{1,0:T(8,128)S(1)}, u32[]{:S(2)}, u32[]{:S(2)}) collective-permute-start(f32[256,128]{1,0:T(8,128)S(1)} %get-tuple-element.33), channel_id=1, source_target_pairs={{1,2},{2,1},{3,4},{4,3},{5,6},{6,5},{7,8},{8,7},{9,10},{10,9},{11,... | collective-permute-start | bytes 393224 | tf_op jit(solution)/shard_map/ppermute | solution.py:524
  8.9 6.8 %collective-permute-start = (f32[256,128]{1,0:T(8,128)S(1)}, f32[256,128]{1,0:T(8,128)S(1)}, u32[]{:S(2)}, u32[]{:S(2)}) collective-permute-start(f32[256,128]{1,0:T(8,128)S(1)} %get-tuple-element.34), channel_id=1, source_target_pairs={{0,1},{1,0},{2,3},{3,2},{4,5},{5,4},{6,7},{7,6},{8,9},{9,8},{10,11... | collective-permute-start | bytes 393224 | tf_op jit(solution)/shard_map/ppermute | solution.py:524
  9.6 0.7 %copy-start.1 = (s32[4096,1]{0,1:T(1,128)S(1)}, s32[4096,1]{0,1:T(1,128)}, u32[]{:S(2)}) copy-start(s32[4096,1]{0,1:T(1,128)} %param.7) | copy-start | bytes 49156
  10.3 0.7 %copy-start.3 = (s32[4096]{0:T(1024)S(1)}, s32[4096]{0:T(1024)}, u32[]{:S(2)}) copy-start(s32[4096]{0:T(1024)} %param.9) | copy-start | bytes 49156
  11.1 0.7 %copy-start.6 = (s32[4096]{0:T(1024)S(1)}, s32[4096]{0:T(1024)}, u32[]{:S(2)}) copy-start(s32[4096]{0:T(1024)} %param.8) | copy-start | bytes 49156
  15.8 19.5 %collective-permute-start.2 = (f32[128,1280]{1,0:T(8,128)S(1)}, f32[128,1280]{1,0:T(8,128)S(1)}, u32[]{:S(2)}, u32[]{:S(2)}) collective-permute-start(f32[128,1280]{1,0:T(8,128)S(1)} %pad_maximum_fusion), channel_id=1, source_target_pairs={{0,32},{32,0},{64,96},{96,64},{1,33},{33,1},{65,97},{97,65},{2,34}... | collective-permute-start | bytes 1966088 | tf_op jit(solution)/shard_map/ppermute | solution.py:524
  17.3 18.1 %collective-permute-start.3 = (f32[128,1280]{1,0:T(8,128)}, f32[128,1280]{1,0:T(8,128)S(1)}, u32[]{:S(2)}, u32[]{:S(2)}) collective-permute-start(f32[128,1280]{1,0:T(8,128)} %pad_maximum_fusion.1), channel_id=1, source_target_pairs={{32,64},{64,32},{33,65},{65,33},{34,66},{66,34},{35,67},{67,35},{3... | collective-permute-start | bytes 1966088 | tf_op jit(solution)/shard_map/ppermute | solution.py:524
  22.6 0.7 copy-start.5
  23.3 12.1 %copy-start.2 = (s32[4096,1]{0,1:T(1,128)S(1)}, s32[4096,1]{0,1:T(1,128)}, u32[]{:S(2)}) copy-start(s32[4096,1]{0,1:T(1,128)} %param.7) | copy-start | bytes 49156
  23.3 12.1 %copy-start.4 = (s32[4096]{0:T(1024)S(1)}, s32[4096]{0:T(1024)}, u32[]{:S(2)}) copy-start(s32[4096]{0:T(1024)} %param.9) | copy-start | bytes 49156
